TPU v7x, 512 devices: a whole 4x4x16 slice. The times are simulated.
512 devices in a mesh: dp: 16 (over x, z_hi, core), seq: 32 (over y, z_lo).
Axes of the slice: x: 4, y: 4, z: 16 (z_hi: 2, z_lo: 8; z = z_hi * 8 + z_lo), core: 2. Of those that a mesh axis runs over, the one named last changes fastest.
Arguments:
- tokens: bfloat16 [16, 32, 128, 1152], P('dp', 'seq'), may hold values from -4 to 4
- spatial_qkv: bfloat16 [16, 32, 128, 3, 576], P('dp', 'seq'), may hold values from -8 to 8
- text_kv: bfloat16 [16, 128, 2, 576], P('dp'), may hold values from -6 to 6
- text_len: int32 [16], P('dp'), may hold values from 1 to 128
- w_os: bfloat16 [576, 1152], P('seq'), may hold values from -0.25 to 0.25
- w_qc: bfloat16 [1152, 576], P('seq'), may hold values from -0.1875 to 0.1875
- w_oc: bfloat16 [576, 1152], P('seq'), may hold values from -0.25 to 0.25
- w_qkv: bfloat16 [1152, 1728], P('seq'), may hold values from -0.1875 to 0.1875
- cotangent: bfloat16 [16, 32, 128, 576], P('dp', None, 'seq'), may hold values from -6 to 6
Outputs:
- temporal_heads: bfloat16 [16, 32, 128, 576], P('dp', None, 'seq')
- grad_tokens: bfloat16 [16, 32, 128, 1152], P('dp', 'seq')
- grad_qkv: bfloat16 [16, 32, 128, 3, 576], P('dp', 'seq')
- grad_os: float32 [576, 1152], P('seq')
All inputs are finite; a program needn't handle non-finite values.
Results may differ from a plain program's by a relative error of at most 0.039.
Values may be sent and summed in bfloat16 or wider, within the bound.
A program may use at most 64 MiB of HBM per device.

v0:
```python
import math

import jax
import jax.numpy as jnp
from jax import lax
from jax.sharding import PartitionSpec as P

HEADS = 8
HEAD = 72


def split_heads(array):
    return array.reshape(array.shape[:-1] + (HEADS, HEAD))


def join_heads(array):
    return array.reshape(array.shape[:-2] + (HEADS * HEAD,))


def times_transposed(left, right):
    return lax.dot_general(
        left, right, (((1,), (1,)), ((), ())), preferred_element_type=jnp.float32
    )


def attend(queries, key_rows, values, score_scale, visible):
    scores = (
        jnp.einsum("bqhe,bkhe->bhqk", queries, key_rows, preferred_element_type=jnp.float32)
        * score_scale
    )
    if visible is not None:
        scores = jnp.where(visible, scores, -1e30)
    weights = jax.nn.softmax(scores, axis=-1)
    output = jnp.einsum(
        "bhqk,bkhe->bqhe", weights.astype(jnp.bfloat16), values, preferred_element_type=jnp.float32
    )
    return (output.astype(jnp.bfloat16), weights)


def attend_grad(upstream, queries, key_rows, values, weights, score_scale, with_memory):
    prob_grad = jnp.einsum("bqhe,bkhe->bhqk", upstream, values, preferred_element_type=jnp.float32)
    score_grad = (
        weights * (prob_grad - jnp.sum(prob_grad * weights, axis=-1, keepdims=True))
    ).astype(jnp.bfloat16)
    query_grad = (
        score_scale
        * jnp.einsum("bhqk,bkhe->bqhe", score_grad, key_rows, preferred_element_type=jnp.float32)
    ).astype(jnp.bfloat16)
    if not with_memory:
        return query_grad
    value_grad = jnp.einsum(
        "bhqk,bqhe->bkhe",
        weights.astype(jnp.bfloat16),
        upstream,
        preferred_element_type=jnp.float32,
    ).astype(jnp.bfloat16)
    key_grad = (
        score_scale
        * jnp.einsum("bhqk,bqhe->bkhe", score_grad, queries, preferred_element_type=jnp.float32)
    ).astype(jnp.bfloat16)
    return (query_grad, key_grad, value_grad)


def shards(tokens, spatial_qkv, text_kv, text_len, w_os, w_qc, w_oc, w_qkv, cotangent):
    frame_count, patch_count, model_width = (tokens.shape[1], tokens.shape[2], tokens.shape[3])
    inner = HEADS * HEAD
    row_count = frame_count * patch_count
    score_scale = 1.0 / math.sqrt(HEAD)
    full_os, full_qc, full_oc, full_qkv = (
        lax.all_gather(w_os, "seq", axis=0, tiled=True),
        lax.all_gather(w_qc, "seq", axis=0, tiled=True),
        lax.all_gather(w_oc, "seq", axis=0, tiled=True),
        lax.all_gather(w_qkv, "seq", axis=0, tiled=True),
    )
    spatial = split_heads(spatial_qkv[0])
    spatial_queries, spatial_keys, spatial_values = (
        spatial[:, :, 0],
        spatial[:, :, 1],
        spatial[:, :, 2],
    )
    spatial_out, spatial_weights = attend(
        spatial_queries, spatial_keys, spatial_values, score_scale, None
    )
    mixed = join_heads(spatial_out).reshape(row_count, inner)
    hidden = (
        tokens[0].reshape(row_count, model_width).astype(jnp.float32)
        + jnp.dot(mixed, full_os, preferred_element_type=jnp.float32)
    ).astype(jnp.bfloat16)
    cross_queries = split_heads(
        jnp.dot(hidden, full_qc, preferred_element_type=jnp.float32).astype(jnp.bfloat16)
    )[None]
    text_keys = split_heads(text_kv[0, :, 0])[None]
    text_values = split_heads(text_kv[0, :, 1])[None]
    visible = jnp.arange(text_kv.shape[1]) < text_len[0]
    cross_out, cross_weights = attend(cross_queries, text_keys, text_values, score_scale, visible)
    after = (
        hidden.astype(jnp.float32)
        + jnp.dot(join_heads(cross_out[0]), full_oc, preferred_element_type=jnp.float32)
    ).astype(jnp.bfloat16)
    patched = lax.all_to_all(
        after.reshape(frame_count, patch_count, model_width),
        "seq",
        split_axis=1,
        concat_axis=0,
        tiled=True,
    )
    all_frames, local_patches = (patched.shape[0], patched.shape[1])
    flat_patched = patched.reshape(all_frames * local_patches, model_width)
    projected = jnp.dot(flat_patched, full_qkv, preferred_element_type=jnp.float32)
    temporal = jnp.swapaxes(
        split_heads(projected.astype(jnp.bfloat16).reshape(all_frames, local_patches, 3, inner)),
        0,
        1,
    )
    temporal_queries, temporal_keys, temporal_values = (
        temporal[:, :, 0],
        temporal[:, :, 1],
        temporal[:, :, 2],
    )
    temporal_out, temporal_weights = attend(
        temporal_queries, temporal_keys, temporal_values, score_scale, None
    )
    temporal_heads = jnp.swapaxes(join_heads(temporal_out), 0, 1)[None]
    upstream = split_heads(jnp.swapaxes(cotangent[0], 0, 1))
    temporal_grads = attend_grad(
        upstream,
        temporal_queries,
        temporal_keys,
        temporal_values,
        temporal_weights,
        score_scale,
        True,
    )
    proj_grad = jnp.swapaxes(jnp.stack(temporal_grads, axis=2), 0, 1).reshape(
        all_frames * local_patches, 3 * inner
    )
    patch_grad = times_transposed(proj_grad, full_qkv)
    patch_grad = patch_grad.astype(jnp.bfloat16).reshape(all_frames, local_patches, model_width)
    after_grad = lax.all_to_all(patch_grad, "seq", split_axis=0, concat_axis=1, tiled=True).reshape(
        row_count, model_width
    )
    cross_grad = split_heads(times_transposed(after_grad, full_oc).astype(jnp.bfloat16))[None]
    cross_query_grad = attend_grad(
        cross_grad, cross_queries, text_keys, text_values, cross_weights, score_scale, False
    )
    hidden_grad = (
        after_grad.astype(jnp.float32) + times_transposed(join_heads(cross_query_grad[0]), full_qc)
    ).astype(jnp.bfloat16)
    mixed_grad = times_transposed(hidden_grad, full_os).astype(jnp.bfloat16)
    partial_grad = lax.dot_general(
        mixed, hidden_grad, (((0,), (0,)), ((), ())), preferred_element_type=jnp.float32
    )
    grad_share = lax.psum_scatter(
        partial_grad.astype(jnp.bfloat16), "seq", scatter_dimension=0, tiled=True
    )
    grad_os = lax.psum(grad_share, "dp").astype(jnp.float32)
    spatial_grads = attend_grad(
        split_heads(mixed_grad.reshape(frame_count, patch_count, inner)),
        spatial_queries,
        spatial_keys,
        spatial_values,
        spatial_weights,
        score_scale,
        True,
    )
    qkv_grad = join_heads(jnp.stack(spatial_grads, axis=2))[None]
    return (
        temporal_heads,
        hidden_grad.reshape(1, frame_count, patch_count, model_width),
        qkv_grad,
        grad_os,
    )


def solution(mesh):
    placed = (
        P("dp", "seq", None, None),
        P("dp", "seq", None, None, None),
        P("dp", None, None, None),
        P("dp"),
        P("seq", None),
        P("seq", None),
        P("seq", None),
        P("seq", None),
        P("dp", None, "seq", None),
    )
    return jax.shard_map(
        shards,
        mesh=mesh,
        in_specs=placed,
        out_specs=(
            P("dp", None, "seq", None),
            P("dp", "seq", None, None),
            P("dp", "seq", None, None, None),
            P("seq", None),
        ),
        check_vma=False,
    )
```

profile of v0, /device:TPU:1, one launch (start us, length us, event | category | flops | bytes accessed | tf_op | source)
XLA Modules:
  0.0 1560.0 jit_solution(209245583571240012)
XLA Ops:
  10.6 2.1 fusion.42
  15.2 205.8 %all-gather.9.cloned.1.call-done = bf16[32,18,1152]{2,1,0:T(8,128)(2,1)} async-done(((bf16[1,18,1152]{2,1,0:T(8,128)(2,1)}), bf16[32,18,1152]{2,1,0:T(8,128)(2,1)}) %all-gather.9.cloned.1.call-update) | async-done | bytes 1327120 | tf_op jit(solution)/shard_map/all_gather | solution.py:70
  220.9 2.4 reshape.196
  223.4 222.6 %all-gather.11.cloned.1.call-done = bf16[32,36,576]{2,1,0:T(8,128)(2,1)} async-done(((bf16[1,36,576]{2,1,0:T(8,128)(2,1)}), bf16[32,36,576]{2,1,0:T(8,128)(2,1)}) %all-gather.11.cloned.1.call-update) | async-done | bytes 1327120 | tf_op jit(solution)/shard_map/all_gather | solution.py:71
  445.9 2.5 reshape.198
  448.5 223.5 %all-gather.13.cloned.1.call-done = bf16[32,18,1152]{2,1,0:T(8,128)(2,1)} async-done(((bf16[1,18,1152]{2,1,0:T(8,128)(2,1)}), bf16[32,18,1152]{2,1,0:T(8,128)(2,1)}) %all-gather.13.cloned.1.call-update) | async-done | bytes 1327120 | tf_op jit(solution)/shard_map/all_gather | solution.py:72
  672.0 3.4 reshape.200
  679.4 1.8 fusion.6
  682.2 3.1 reduce.12
  685.3 1.9 reshape.204
  687.2 10.0 all-to-all-start
  698.2 14.1 all-to-all-done
  712.2 2.3 reshape.205
  714.5 197.5 %all-gather.15.cloned.1.call-done = bf16[32,36,1728]{2,1,0:T(8,128)(2,1)} async-done(((bf16[1,36,1728]{2,1,0:T(8,128)(2,1)}), bf16[32,36,1728]{2,1,0:T(8,128)(2,1)}) %all-gather.15.cloned.1.call-update) | async-done | bytes 3981328 | tf_op jit(solution)/shard_map/all_gather | solution.py:73
  912.0 7.3 reshape.202
  919.3 4.6 convolution_convert_fusion.2
  926.9 2.3 copy.92
  934.4 1.9 reshape.188
  936.3 3.6 convolution_convert_fusion.1
  940.6 9.5 all-to-all-start.1
  954.8 10.6 all-to-all-done.1
  965.4 1.9 convolution_convert_fusion.9
  975.7 442.7 %all-reduce.3.cloned.1.call-done = bf16[576,1152]{1,0:T(8,128)(2,1)} async-done(((bf16[576,1152]{1,0:T(8,128)(2,1)}), bf16[576,1152]{1,0:T(8,128)(2,1)}) %all-reduce.3.cloned.1.call-update) | async-done | bytes 1327120
  1419.3 133.4 %psum.7 = bf16[18,1152]{1,0:T(8,128)(2,1)S(1)} all-reduce(bf16[18,1152]{1,0:T(8,128)(2,1)S(1)} %constant_dynamic-slice_fusion), channel_id=1, replica_groups=mesh['dp'=16,'seq'=32] {'dp'}, use_global_device_ids=true, to_apply=%region_10.11 | all-reduce | flops 20736 | bytes 82944 | tf_op jit(solution)/shard_map/psum | solution.py:156
  (98 shorter events, 33.8 us)
Async XLA Ops:
  7.2 213.8 %all-gather.9.cloned.1.call-start = ((), (), s32[]{:S(2)}) async-start(), calls=%async_computation.2 | async-start | bytes 1824768 | tf_op jit(solution)/shard_map/all_gather | solution.py:70
  7.9 438.0 %all-gather.11.cloned.1.call-start = ((), (), s32[]{:S(2)}) async-start(), calls=%async_computation.3 | async-start | bytes 1689600 | tf_op jit(solution)/shard_map/all_gather | solution.py:71
  8.6 663.3 %all-gather.13.cloned.1.call-start = ((), (), s32[]{:S(2)}) async-start(), calls=%async_computation.4 | async-start | bytes 1824768 | tf_op jit(solution)/shard_map/all_gather | solution.py:72
  9.4 902.6 %all-gather.15.cloned.1.call-start = ((), (), s32[]{:S(2)}) async-start(), calls=%async_computation.5 | async-start | bytes 4730880 | tf_op jit(solution)/shard_map/all_gather | solution.py:73
  10.6 667.4 %copy-start.19 = (pred[128]{0:T(512)(128)(4,1)}, pred[128]{0:T(512)(128)(4,1)S(1)}, u32[]{:S(2)}) copy-start(pred[128]{0:T(512)(128)(4,1)S(1)} %iota_compare_fusion) | copy-start | bytes 388
  12.7 2.4 copy-start.17
  12.8 1.6 copy-start.6
  14.4 661.1 %copy-start.2 = (bf16[8,128,72]{1,2,0:T(8,128)(2,1)}, bf16[8,128,72]{1,2,0:T(8,128)(2,1)S(1)}, u32[]{:S(2)}) copy-start(bf16[8,128,72]{1,2,0:T(8,128)(2,1)S(1)} %convolution_convert_fusion.7) | copy-start | bytes 442372
  448.4 227.0 %copy-start.7 = (bf16[1,1,128,1152]{3,2,1,0:T(8,128)(2,1)S(1)}, bf16[1,1,128,1152]{3,2,1,0:T(8,128)(2,1)}, u32[]{:S(2)}) copy-start(bf16[1,1,128,1152]{3,2,1,0:T(8,128)(2,1)} %param.9) | copy-start | bytes 884740
  675.9 2.1 copy-start.13
  678.0 1.4 copy-start.22
  681.2 15.9 %copy-start.10 = (bf16[1,32,4,576]{3,2,1,0:T(4,128)(2,1)S(1)}, bf16[1,32,4,576]{3,2,1,0:T(4,128)(2,1)}, u32[]{:S(2)}) copy-start(bf16[1,32,4,576]{3,2,1,0:T(4,128)(2,1)} %param.17) | copy-start | bytes 442372
  687.2 25.0 %all-to-all-start = ((bf16[32,2,2304]{2,1,0:T(2,128)(2,1)}), bf16[32,2,2304]{2,1,0:T(2,128)(2,1)}, u32[]{:S(2)}, u32[]{:S(2)}) async-start(bf16[32,2,2304]{2,1,0:T(2,128)(2,1)} %reshape.204), calls=%async_computation | async-start | bytes 589824 | tf_op jit(solution)/shard_map/all_to_all | solution.py:100
  930.6 1.8 copy-start.5
  930.6 1.8 copy-start.16
  930.6 1.5 copy-start.8
  940.6 24.7 %all-to-all-start.1 = ((bf16[32,4,1152]{2,1,0:T(4,128)(2,1)}), bf16[32,4,1152]{2,1,0:T(4,128)(2,1)S(1)}, u32[]{:S(2)}, u32[]{:S(2)}) async-start(bf16[32,4,1152]{2,1,0:T(4,128)(2,1)} %reshape.189), calls=%async_computation.1 | async-start | bytes 589824 | tf_op jit(solution)/shard_map/all_to_all | solution.py:139
  950.1 468.3 %all-reduce.3.cloned.1.call-start = ((), (), s32[]{:S(2)}) async-start(), calls=%async_computation.6 | async-start | bytes 2654208
  953.8 13.5 copy-start.23
  954.8 12.6 copy-start.14
  965.4 1.9 copy-start.21
  970.8 2.1 copy-start
  971.3 1.6 copy-start.9
  971.3 1.6 copy-start.18
  (7 other events, 8.2 us)
Sparse Core Ops, SparseCore 0:
  10.1 210.8 all-gather.8
  223.0 222.8 all-gather.10
  448.0 223.9 all-gather.12
  673.9 238.0 all-gather.14
  973.0 445.3 all-reduce.2
where the time goes:
time: 1570 us; the launch traced here: 1560 us
  waiting for transfers between devices  1320 us (84%)
  blocking collectives  133 us (8%)
  local copies, waits for them, and re-layouts  35.8 us (2%)
  matrix products  31 us (2%)
  starting transfers between devices  19.8 us (1%)
    unnamed x6, waiting for transfers between devices  445 us
    all_gather x1, waiting for transfers between devices, shards(): lax.all_gather(w_oc, 'seq', axis=0, tiled=True)  224 us
    all_gather x1, waiting for transfers between devices, shards(): lax.all_gather(w_qc, 'seq', axis=0, tiled=True)  223 us
    all_gather x1, waiting for transfers between devices, shards(): lax.all_gather(w_os, 'seq', axis=0, tiled=True)  206 us
    all_gather x1, waiting for transfers between devices, shards(): lax.all_gather(w_qkv, 'seq', axis=0, tiled=True)  198 us
    psum x1, blocking collectives, shards(): grad_os = lax.psum(grad_share, 'dp').astype(jnp.float32)  133 us
  transfers between devices with their start and end apart: 7, of which 7 were waited for; matrix products, arithmetic and copies ran while one was open for 2% of the time, Pallas kernels for 0%

commit v1 on v0

--- a/solution.py
+++ b/solution.py
@@ -1,12 +1,202 @@
+import functools
 import math
 
 import jax
 import jax.numpy as jnp
 from jax import lax
+from jax.experimental import pallas as pl
+from jax.experimental.pallas import tpu as pltpu
 from jax.sharding import PartitionSpec as P
 
 HEADS = 8
 HEAD = 72
+MESH = pl.DeviceIdType.MESH
+BF16 = jnp.bfloat16
+F32 = jnp.float32
+SHARDS = ((18, 32, 1152, 80), (36, 48, 576, 144), (18, 32, 1152, 80), (36, 48, 1728, 144))
+
+
+def place():
+    dp, seq = lax.axis_index("dp"), lax.axis_index("seq")
+    return lax.rem(dp, 2), lax.div(dp, 4), lax.div(seq, 8), lax.rem(lax.div(dp, 2), 2) * 8 + lax.rem(seq, 8)
+
+
+def device(core, x, y, z):
+    return ((x * 2 + lax.div(z, 8)) * 2 + core, y * 8 + lax.rem(z, 8))
+
+
+class Gather:
+    def __init__(self, shards, landing, full, sems):
+        self.shards, self.landing, self.full = shards, landing, full
+        (self.zs, self.zr, self.ps, self.pr, self.ys, self.yr, self.qs, self.qr) = sems
+        core, x, y, z = place()
+        self.core, self.y, self.slot = core, y, lax.rem(z, 8)
+        self.step = 1 - 2 * core
+        self.next_z = device(core, x, y, lax.rem(z + self.step + 16, 16))
+        self.prev_z = device(core, x, y, lax.rem(z - self.step + 16, 16))
+        self.next_y = device(core, x, lax.rem(y + self.step + 4, 4), z)
+        self.prev_y = device(core, x, lax.rem(y - self.step + 4, 4), z)
+        self.partner = device(1 - core, x, y, z)
+
+    def neighbours(self):
+        return (self.next_z, self.prev_z, self.next_y, self.prev_y, self.partner)
+
+    def stage(self, w):
+        rows = SHARDS[w][0]
+        block = self.landing[w]
+        block[self.slot] = jnp.zeros(block.shape[1:], BF16)
+        block[self.slot, 0:rows, :] = self.shards[w][...]
+
+    def z_copy(self, w, s, slot):
+        block = self.landing[w].at[slot]
+        return pltpu.make_async_remote_copy(
+            src_ref=block, dst_ref=block, send_sem=self.zs.at[w, s], recv_sem=self.zr.at[w, s],
+            device_id=self.next_z, device_id_type=MESH)
+
+    def pass_copy(self, w, s, slot):
+        block = self.landing[w].at[slot]
+        return pltpu.make_async_remote_copy(
+            src_ref=block, dst_ref=block, send_sem=self.ps.at[w, s], recv_sem=self.pr.at[w, s],
+            device_id=self.partner, device_id_type=MESH)
+
+    def away(self, steps):
+        return lax.rem(self.slot - steps * self.step + 8, 8)
+
+    def z_start(self, w):
+        self.z_copy(w, 0, self.slot).start()
+
+    def z_step(self, w, s):
+        def go():
+            slot = self.away(s + 1)
+            self.z_copy(w, s, slot).wait_recv()
+            if s < 2:
+                self.z_copy(w, s + 1, slot).start()
+            if s == 2:
+                pl.when(self.core == 0)(lambda: self.z_copy(w, 3, slot).start())
+            self.pass_copy(w, s, slot).start()
+
+        if s < 3:
+            go()
+        else:
+            pl.when(self.core == 0)(go)
+
+    def z_finish(self, w):
+        for s in range(3):
+            self.pass_copy(w, s, lax.rem(self.slot + (s + 1) * self.step + 8, 8)).wait_recv()
+        pl.when(self.core == 1)(
+            lambda: self.pass_copy(w, 3, lax.rem(self.slot + 4, 8)).wait_recv())
+        rows = SHARDS[w][0]
+        for k in range(8):
+            self.full[w][self.y, k * rows:(k + 1) * rows, :] = self.landing[w][k, 0:rows, :]
+
+    def y_copy(self, w, s, quarter, part, to, send, recv):
+        block = self.full[w].at[quarter] if part is None else self.full[w].at[quarter, pl.ds(*part)]
+        return pltpu.make_async_remote_copy(
+            src_ref=block, dst_ref=block, send_sem=send.at[w, s], recv_sem=recv.at[w, s],
+            device_id=to, device_id_type=MESH)
+
+    def parts(self, w):
+        cut, rows = SHARDS[w][3], SHARDS[w][0] * 8
+        return ((0, cut), (cut, rows - cut))
+
+    def y_start(self, w):
+        self.y_copy(w, 0, self.y, None, self.next_y, self.ys, self.yr).start()
+
+    def y_step(self, w):
+        quarter = lax.rem(self.y - self.step + 4, 4)
+        self.y_copy(w, 0, quarter, None, self.next_y, self.ys, self.yr).wait_recv()
+        for c in range(2):
+            pl.when(self.core == c)(
+                lambda: self.y_copy(w, 1, quarter, self.parts(w)[c], self.next_y, self.ys, self.yr).start())
+        self.y_copy(w, 0, quarter, None, self.partner, self.qs, self.qr).start()
+
+    def y_last(self, w):
+        quarter = lax.rem(self.y + 2, 4)
+        for c in range(2):
+            def go():
+                self.y_copy(w, 1, quarter, self.parts(w)[c], self.next_y, self.ys, self.yr).wait_recv()
+                self.y_copy(w, 1, quarter, self.parts(w)[c], self.partner, self.qs, self.qr).start()
+            pl.when(self.core == c)(go)
+
+    def y_finish(self, w):
+        quarter = lax.rem(self.y + self.step + 4, 4)
+        self.y_copy(w, 0, quarter, None, self.partner, self.qs, self.qr).wait_recv()
+        far = lax.rem(self.y + 2, 4)
+        for c in range(2):
+            pl.when(self.core == c)(
+                lambda: self.y_copy(w, 1, far, self.parts(w)[1 - c], self.partner, self.qs, self.qr).wait_recv())
+
+    def drain(self, w):
+        for s in range(3):
+            self.z_copy(w, s, self.away(s)).wait_send()
+            self.pass_copy(w, s, self.away(s + 1)).wait_send()
+
+        def last():
+            self.z_copy(w, 3, self.away(3)).wait_send()
+            self.pass_copy(w, 3, self.away(4)).wait_send()
+
+        pl.when(self.core == 0)(last)
+        self.y_copy(w, 0, self.y, None, self.next_y, self.ys, self.yr).wait_send()
+        quarter = lax.rem(self.y - self.step + 4, 4)
+        self.y_copy(w, 0, quarter, None, self.partner, self.qs, self.qr).wait_send()
+        far = lax.rem(self.y + 2, 4)
+        for c in range(2):
+            def go():
+                self.y_copy(w, 1, quarter, self.parts(w)[c], self.next_y, self.ys, self.yr).wait_send()
+                self.y_copy(w, 1, far, self.parts(w)[c], self.partner, self.qs, self.qr).wait_send()
+            pl.when(self.core == c)(go)
+
+
+def gather_kernel(*refs):
+    shards, full, landing, sems = refs[0:4], refs[4:8], refs[8:12], refs[12:20]
+    g = Gather(shards, landing, full, sems)
+    barrier = pltpu.get_barrier_semaphore()
+    for d in g.neighbours():
+        pl.semaphore_signal(barrier, inc=1, device_id=d, device_id_type=MESH)
+    for w in range(4):
+        g.stage(w)
+    pl.semaphore_wait(barrier, 5)
+    first = (0, 1, 2)
+    for w in first:
+        g.z_start(w)
+    for s in range(4):
+        for w in first:
+            g.z_step(w, s)
+    g.z_start(3)
+    for w in first:
+        g.z_finish(w)
+        g.y_start(w)
+    for s in range(4):
+        g.z_step(3, s)
+        if s < 3:
+            g.y_step(s)
+    g.z_finish(3)
+    g.y_start(3)
+    for w in first:
+        g.y_last(w)
+    for w in first:
+        g.y_finish(w)
+    g.y_step(3)
+    g.y_last(3)
+    g.y_finish(3)
+    for w in range(4):
+        g.drain(w)
+
+
+def gather_weights(*shards):
+    vmem = pl.BlockSpec(memory_space=pltpu.VMEM)
+    out = pl.pallas_call(
+        gather_kernel,
+        out_shape=[jax.ShapeDtypeStruct((4, rows * 8, columns), BF16) for rows, _, columns, _ in SHARDS],
+        in_specs=[vmem] * 4,
+        out_specs=[vmem] * 4,
+        scratch_shapes=[pltpu.VMEM((8, padded, columns), BF16) for _, padded, columns, _ in SHARDS]
+        + [pltpu.SemaphoreType.DMA((4, 4))] * 4 + [pltpu.SemaphoreType.DMA((4, 2))] * 4,
+        compiler_params=pltpu.CompilerParams(
+            collective_id=0, has_side_effects=True, vmem_limit_bytes=48 * 2**20),
+        name="gather_weights",
+    )(*shards)
+    return [o.reshape(-1, o.shape[-1]) for o in out]
 
 
 def split_heads(array):
@@ -66,12 +256,7 @@
     inner = HEADS * HEAD
     row_count = frame_count * patch_count
     score_scale = 1.0 / math.sqrt(HEAD)
-    full_os, full_qc, full_oc, full_qkv = (
-        lax.all_gather(w_os, "seq", axis=0, tiled=True),
-        lax.all_gather(w_qc, "seq", axis=0, tiled=True),
-        lax.all_gather(w_oc, "seq", axis=0, tiled=True),
-        lax.all_gather(w_qkv, "seq", axis=0, tiled=True),
-    )
+    full_os, full_qc, full_oc, full_qkv = gather_weights(w_os, w_qc, w_oc, w_qkv)
     spatial = split_heads(spatial_qkv[0])
     spatial_queries, spatial_keys, spatial_values = (
         spatial[:, :, 0],

time: 1570 us -> 761 us (0.48)
  waiting for transfers between devices: 1320 us -> 458 us
  Pallas kernels: 0 us -> 73.3 us
    all_gather x4 -> x0, waiting for transfers between devices: 849 us -> none  [the longest x1 224 us: shards(): lax.all_gather(w_oc, 'seq', axis=0, tiled=True)]
    pallas_call x0 -> x1, Pallas kernels: none -> 73.3 us  [gather_weights(): pl.pallas_call(gather_kernel, out_shape=[jax.ShapeDtypeStruct((4, rows *...]
    unnamed x6 -> x2, waiting for transfers between devices: 445 us -> 423 us
  transfers between devices with their start and end apart: 7 -> 3, of which waited for: 7 -> 3; matrix products, arithmetic and copies ran while one was open for 2% -> 1% of each run, Pallas kernels for 0% -> 0%
where the time goes in v1:
time: 761 us; the launch traced here: 751 us
  waiting for transfers between devices  458 us (60%)
  blocking collectives  133 us (17%)
  Pallas kernels  73.3 us (10%)
  matrix products  31.4 us (4%)
  local copies, waits for them, and re-layouts  21.5 us (3%)
  between operations  15.8 us (2%)
  starting transfers between devices  12.1 us (2%)
    unnamed x2, waiting for transfers between devices  423 us
    psum x1, blocking collectives, shards(): grad_os = lax.psum(grad_share, 'dp').astype(jnp.float32)  133 us
    pallas_call x1, Pallas kernels, gather_weights(): pl.pallas_call(gather_kernel, out_shape=[jax.ShapeDtypeStruct((4, rows *...  73.3 us
    all_to_all x1, waiting for transfers between devices, shards(): lax.all_to_all(after.reshape(frame_count, patch_count, model_width), 'seq...  19 us
    all_to_all x1, waiting for transfers between devices, shards(): lax.all_to_all(patch_grad, 'seq', split_axis=0, concat_axis=1, tiled=True)  15.7 us
  transfers between devices with their start and end apart: 3, of which 3 were waited for; matrix products, arithmetic and copies ran while one was open for 1% of the time, Pallas kernels for 0%

profile of v1, /device:TPU:1, one launch (start us, length us, event | category | flops | bytes accessed | tf_op | source)
XLA Modules:
  0.0 750.9 jit_solution(10837556484189903290)
XLA Ops:
  7.2 1.8 fusion.41
  9.0 2.1 fusion.42
  12.9 73.3 %gather_weights.1 = (bf16[4,144,1152]{2,1,0:T(8,128)(2,1)S(1)}, bf16[4,288,576]{2,1,0:T(8,128)(2,1)S(1)}, bf16[4,144,1152]{2,1,0:T(8,128)(2,1)S(1)}, bf16[4,288,1728]{2,1,0:T(8,128)(2,1)}) custom-call(bf16[18,1152]{1,0:T(8,128)(2,1)S(1)} %copy-done.2, bf16[36,576]{1,0:T(8,128)(2,1)S(1)} %copy-done.4, bf16[18,1152]{1,0:T(8,128)(2,1)S(1)} %copy-done.3, ...), custom_call_target="tpu_custom_call" | custom-call | tf_op jit(solution)/shard_map/gather_weights/pallas_call | solution.py:188
  88.0 2.1 fusion.43
  90.1 1.4 convolution_convert_fusion.6
  91.5 1.8 fusion.6
  94.3 3.1 reduce.12
  97.4 1.9 reshape.212
  99.3 6.9 all-to-all-start
  107.2 19.0 %all-to-all-done = bf16[32,2,2304]{2,1,0:T(2,128)(2,1)} async-done(((bf16[32,2,2304]{2,1,0:T(2,128)(2,1)}), bf16[32,2,2304]{2,1,0:T(2,128)(2,1)}, u32[]{:S(2)}, u32[]{:S(2)}) %all-to-all-start) | async-done | bytes 294944 | tf_op jit(solution)/shard_map/all_to_all | solution.py:285
  126.2 2.3 reshape.213
  128.5 4.6 convolution_convert_fusion.2
  134.3 1.7 reshape_reshape.8
  136.1 2.4 copy.92
  139.9 1.4 fusion.19
  143.6 1.9 reshape.204
  145.5 3.6 convolution_convert_fusion.1
  149.9 5.2 all-to-all-start.1
  159.5 15.7 %all-to-all-done.1 = bf16[32,4,1152]{2,1,0:T(4,128)(2,1)S(1)} async-done(((bf16[32,4,1152]{2,1,0:T(4,128)(2,1)}), bf16[32,4,1152]{2,1,0:T(4,128)(2,1)S(1)}, u32[]{:S(2)}, u32[]{:S(2)}) %all-to-all-start.1) | async-done | bytes 294944 | tf_op jit(solution)/shard_map/all_to_all | solution.py:324
  175.3 1.9 convolution_convert_fusion.9
  178.3 1.6 fusion.20
  181.6 1.6 convolution_convert_fusion
  186.0 423.1 %all-reduce.3.cloned.1.call-done = bf16[576,1152]{1,0:T(8,128)(2,1)} async-done(((bf16[576,1152]{1,0:T(8,128)(2,1)}), bf16[576,1152]{1,0:T(8,128)(2,1)}) %all-reduce.3.cloned.1.call-update) | async-done | bytes 1327120
  610.0 133.4 %psum.7 = bf16[18,1152]{1,0:T(8,128)(2,1)S(1)} all-reduce(bf16[18,1152]{1,0:T(8,128)(2,1)S(1)} %constant_dynamic-slice_fusion), channel_id=1, replica_groups=mesh['dp'=16,'seq'=32] {'dp'}, use_global_device_ids=true, to_apply=%region_10.11 | all-reduce | flops 20736 | bytes 82944 | tf_op jit(solution)/shard_map/psum | solution.py:341
  (93 shorter events, 21.4 us)
Async XLA Ops:
  7.2 3.9 copy-start.13
  11.1 1.8 copy-start.1
  11.1 1.8 copy-start.2
  11.1 1.8 copy-start.3
  11.1 1.7 copy-start.4
  11.1 75.1 %copy-start.11 = (bf16[1,1,128,1152]{3,2,1,0:T(8,128)(2,1)S(1)}, bf16[1,1,128,1152]{3,2,1,0:T(8,128)(2,1)}, u32[]{:S(2)}) copy-start(bf16[1,1,128,1152]{3,2,1,0:T(8,128)(2,1)} %param.9) | copy-start | bytes 884740
  11.7 76.4 %copy-start.7 = (bf16[8,128,72]{1,2,0:T(8,128)(2,1)}, bf16[8,128,72]{1,2,0:T(8,128)(2,1)S(1)}, u32[]{:S(2)}) copy-start(bf16[8,128,72]{1,2,0:T(8,128)(2,1)S(1)} %convolution_convert_fusion.7) | copy-start | bytes 442372
  86.2 1.8 copy-start
  86.7 3.4 copy-start.18
  90.1 1.4 copy-start.27
  93.3 12.9 %copy-start.15 = (bf16[1,32,4,576]{3,2,1,0:T(4,128)(2,1)S(1)}, bf16[1,32,4,576]{3,2,1,0:T(4,128)(2,1)}, u32[]{:S(2)}) copy-start(bf16[1,32,4,576]{3,2,1,0:T(4,128)(2,1)} %param.17) | copy-start | bytes 442372
  99.3 27.0 %all-to-all-start = ((bf16[32,2,2304]{2,1,0:T(2,128)(2,1)}), bf16[32,2,2304]{2,1,0:T(2,128)(2,1)}, u32[]{:S(2)}, u32[]{:S(2)}) async-start(bf16[32,2,2304]{2,1,0:T(2,128)(2,1)} %reshape.212), calls=%async_computation | async-start | bytes 589824 | tf_op jit(solution)/shard_map/all_to_all | solution.py:285
  139.8 1.8 copy-start.10
  139.8 1.8 copy-start.21
  139.8 1.4 copy-start.6
  139.8 1.5 copy-start.12
  149.9 25.3 %all-to-all-start.1 = ((bf16[32,4,1152]{2,1,0:T(4,128)(2,1)}), bf16[32,4,1152]{2,1,0:T(4,128)(2,1)S(1)}, u32[]{:S(2)}, u32[]{:S(2)}) async-start(bf16[32,4,1152]{2,1,0:T(4,128)(2,1)} %reshape.205), calls=%async_computation.1 | async-start | bytes 589824 | tf_op jit(solution)/shard_map/all_to_all | solution.py:324
  155.1 454.0 %all-reduce.3.cloned.1.call-start = ((), (), s32[]{:S(2)}) async-start(), calls=%async_computation.2 | async-start | bytes 2654208
  158.8 18.4 %copy-start.28 = (f32[8,128]{1,0:T(8,128)S(1)}, f32[8,128]{1,0:T(8,128)}, u32[]{:S(2)}) copy-start(f32[8,128]{1,0:T(8,128)} %copy-done.27) | copy-start | bytes 12292
  159.5 17.7 %copy-start.19 = (bf16[1,128,1,576]{1,3,2,0:T(8,128)(2,1)S(1)}, bf16[1,128,1,576]{1,3,2,0:T(8,128)(2,1)}, u32[]{:S(2)}) copy-start(bf16[1,128,1,576]{1,3,2,0:T(8,128)(2,1)} %get-tuple-element.25) | copy-start | bytes 442372
  175.3 2.0 copy-start.26
  180.5 2.6 copy-start.5
  181.6 1.6 copy-start.14
  181.6 1.6 copy-start.23
  (8 other events, 8.8 us)
Sparse Core Ops, SparseCore 0:
  183.3 425.7 all-reduce.2

commit v2 on v1

--- a/solution.py
+++ b/solution.py
@@ -199,6 +199,203 @@
     return [o.reshape(-1, o.shape[-1]) for o in out]
 
 
+class Reduce:
+    def __init__(self, partial, taken, pieces, plane, total, z_out, z_in, x_out, x_in, sems):
+        self.partial, self.taken, self.pieces, self.plane = partial, taken, pieces, plane
+        self.total, self.z_out, self.z_in, self.x_out, self.x_in = total, z_out, z_in, x_out, x_in
+        (self.cs, self.cr, self.ps, self.pr, self.zs, self.zr, self.xs, self.xr) = sems
+        self.core, self.x, self.y, self.z = place()
+        self.holds = jnp.logical_and(self.x < 3, lax.div(self.y, 2) == self.core)
+        self.me = self.x * 4 + self.y
+
+    def greet(self, barrier):
+        def signal(d):
+            pl.semaphore_signal(barrier, inc=1, device_id=d, device_id_type=MESH)
+
+        core, x, y, z = self.core, self.x, self.y, self.z
+
+        @pl.loop(1, 16)
+        def _(k):
+            signal(device(core, lax.rem(x + lax.div(k, 4), 4), lax.rem(y + lax.rem(k, 4), 4), z))
+            signal(device(core, x, y, lax.rem(z + k, 16)))
+
+        @pl.loop(0, 4)
+        def _(k):
+            signal(device(1 - core, lax.rem(x + k, 4), y, z))
+
+        return 34
+
+    def core_copy(self):
+        return pltpu.make_async_remote_copy(
+            src_ref=self.partial.at[1 - self.core], dst_ref=self.taken, send_sem=self.cs, recv_sem=self.cr,
+            device_id=device(1 - self.core, self.x, self.y, self.z), device_id_type=MESH)
+
+    def plane_copy(self, upper, x):
+        return pltpu.make_async_remote_copy(
+            src_ref=self.pieces.at[upper, x], dst_ref=self.plane.at[self.me],
+            send_sem=self.ps.at[upper * 3 + x], recv_sem=self.pr.at[self.me],
+            device_id=device(self.core, x, self.core * 2 + upper, self.z), device_id_type=MESH)
+
+    def is_me(self, upper, x):
+        return jnp.logical_and(self.x == x, self.y == self.core * 2 + upper)
+
+    def plane_start(self):
+        self.core_copy().wait_recv()
+        for upper in range(2):
+            for x in range(3):
+                rows, columns = slice(144 * upper, 144 * upper + 144), slice(384 * x, 384 * x + 384)
+                self.pieces[upper, x] = (
+                    self.partial[self.core, rows, columns].astype(F32)
+                    + self.taken[rows, columns].astype(F32)).astype(BF16)
+        for upper in range(2):
+            for x in range(3):
+                pl.when(jnp.logical_not(self.is_me(upper, x)))(
+                    lambda: self.plane_copy(upper, x).start())
+
+                @pl.when(self.is_me(upper, x))
+                def _():
+                    self.plane[self.me] = self.pieces[upper, x]
+
+    def z_copy(self, k):
+        to = lax.rem(self.z + k, 16)
+        return pltpu.make_async_remote_copy(
+            src_ref=self.z_out.at[lax.rem(to, 8)], dst_ref=self.z_in.at[self.z],
+            send_sem=self.zs.at[k], recv_sem=self.zr.at[self.z],
+            device_id=device(self.core, self.x, self.y, to), device_id_type=MESH)
+
+    def z_start(self):
+        @pl.when(self.holds)
+        def _():
+            @pl.loop(0, 16)
+            def _(k):
+                @pl.when(k != self.me)
+                def _():
+                    block = self.plane.at[k]
+                    pltpu.make_async_remote_copy(
+                        src_ref=block, dst_ref=block, send_sem=self.ps.at[0], recv_sem=self.pr.at[k],
+                        device_id=device(1 - self.core, self.x, self.y, self.z), device_id_type=MESH).wait_recv()
+
+            for r in range(3):
+                rows = slice(48 * r, 48 * r + 48)
+                sum_rows = self.plane[0, rows].astype(F32)
+                for k in range(1, 16):
+                    sum_rows = sum_rows + self.plane[k, rows].astype(F32)
+                self.total[rows] = sum_rows
+            self.z_out[...] = jnp.zeros(self.z_out.shape, BF16)
+            for k in range(8):
+                self.z_out[k, 0:18, :] = self.total[18 * k:18 * k + 18, :].astype(BF16)
+
+            @pl.loop(1, 16)
+            def _(k):
+                self.z_copy(k).start()
+
+            self.z_in[self.z] = self.z_out[lax.rem(self.z, 8)]
+
+    def x_copy(self, k):
+        other = lax.div(k, 4)
+        return pltpu.make_async_remote_copy(
+            src_ref=self.x_out, dst_ref=self.x_in.at[self.x],
+            send_sem=self.xs.at[k], recv_sem=self.xr.at[self.x],
+            device_id=device(lax.rem(self.core + other, 2), lax.rem(self.x + k, 4), self.y, self.z),
+            device_id_type=MESH)
+
+    def x_start(self):
+        @pl.when(self.holds)
+        def _():
+            @pl.loop(0, 16)
+            def _(k):
+                @pl.when(k != self.z)
+                def _():
+                    block = self.z_in.at[k]
+                    pltpu.make_async_remote_copy(
+                        src_ref=block, dst_ref=block, send_sem=self.zs.at[0], recv_sem=self.zr.at[k],
+                        device_id=device(1 - self.core, self.x, self.y, self.z), device_id_type=MESH).wait_recv()
+
+            sum_rows = self.z_in[0].astype(F32)
+            for k in range(1, 16):
+                sum_rows = sum_rows + self.z_in[k].astype(F32)
+            self.x_out[...] = sum_rows.astype(BF16)
+
+            @pl.loop(1, 8)
+            def _(k):
+                self.x_copy(k).start()
+
+            self.x_in[self.x] = self.x_out[...]
+
+    def finish(self, out):
+        for k in range(3):
+            @pl.when(jnp.logical_not(jnp.logical_and(self.holds, self.x == k)))
+            def _():
+                block = self.x_in.at[k]
+                pltpu.make_async_remote_copy(
+                    src_ref=block, dst_ref=block, send_sem=self.xs.at[0], recv_sem=self.xr.at[k],
+                    device_id=device(1 - self.core, self.x, self.y, self.z), device_id_type=MESH).wait_recv()
+            out[:, 384 * k:384 * k + 384] = self.x_in[k, 0:18, :].astype(F32)
+
+    def drain(self):
+        self.core_copy().wait_send()
+        for upper in range(2):
+            for x in range(3):
+                pl.when(jnp.logical_not(self.is_me(upper, x)))(
+                    lambda: self.plane_copy(upper, x).wait_send())
+
+        @pl.when(self.holds)
+        def _():
+            @pl.loop(1, 16)
+            def _(k):
+                self.z_copy(k).wait_send()
+
+            @pl.loop(1, 8)
+            def _(k):
+                self.x_copy(k).wait_send()
+
+
+REDUCE_SCRATCH = [
+    pltpu.VMEM((2, 288, 1152), BF16),
+    pltpu.VMEM((288, 1152), BF16),
+    pltpu.VMEM((2, 3, 144, 384), BF16),
+    pltpu.VMEM((16, 144, 384), BF16),
+    pltpu.VMEM((144, 384), F32),
+    pltpu.VMEM((8, 32, 384), BF16),
+    pltpu.VMEM((16, 32, 384), BF16),
+    pltpu.VMEM((32, 384), BF16),
+    pltpu.VMEM((3, 32, 384), BF16),
+]
+REDUCE_SEMS = [pltpu.SemaphoreType.DMA, pltpu.SemaphoreType.DMA] + [
+    pltpu.SemaphoreType.DMA((n,)) for n in (6, 16, 16, 16, 8, 3)]
+
+
+def reduce_kernel(*refs):
+    mixed_t, grad, out = refs[0:3]
+    r = Reduce(*refs[3:12], refs[12:20])
+    barrier = pltpu.get_barrier_semaphore()
+    count = r.greet(barrier)
+    for half in range(2):
+        r.partial[half] = jnp.dot(
+            mixed_t[288 * half:288 * half + 288, :], grad[...], preferred_element_type=F32).astype(BF16)
+    pl.semaphore_wait(barrier, count)
+    r.core_copy().start()
+    r.plane_start()
+    r.z_start()
+    r.x_start()
+    r.finish(out)
+    r.drain()
+
+
+def reduce_grad(mixed_t, grad):
+    vmem = pl.BlockSpec(memory_space=pltpu.VMEM)
+    return pl.pallas_call(
+        reduce_kernel,
+        out_shape=jax.ShapeDtypeStruct((18, 1152), F32),
+        in_specs=[vmem] * 2,
+        out_specs=vmem,
+        scratch_shapes=REDUCE_SCRATCH + REDUCE_SEMS,
+        compiler_params=pltpu.CompilerParams(
+            collective_id=1, has_side_effects=True, vmem_limit_bytes=48 * 2**20),
+        name="reduce_grad",
+    )(mixed_t, grad)
+
+
 def split_heads(array):
     return array.reshape(array.shape[:-1] + (HEADS, HEAD))
 
@@ -332,13 +529,7 @@
         after_grad.astype(jnp.float32) + times_transposed(join_heads(cross_query_grad[0]), full_qc)
     ).astype(jnp.bfloat16)
     mixed_grad = times_transposed(hidden_grad, full_os).astype(jnp.bfloat16)
-    partial_grad = lax.dot_general(
-        mixed, hidden_grad, (((0,), (0,)), ((), ())), preferred_element_type=jnp.float32
-    )
-    grad_share = lax.psum_scatter(
-        partial_grad.astype(jnp.bfloat16), "seq", scatter_dimension=0, tiled=True
-    )
-    grad_os = lax.psum(grad_share, "dp").astype(jnp.float32)
+    grad_os = reduce_grad(mixed.T, hidden_grad)
     spatial_grads = attend_grad(
         split_heads(mixed_grad.reshape(frame_count, patch_count, inner)),
         spatial_queries,

time: 761 us -> 225 us (0.30); the launches traced: 751 us -> 224 us
  waiting for transfers between devices: 458 us -> 34 us
  blocking collectives: 133 us -> 0 us
  Pallas kernels: 73.3 us -> 116 us
  between operations: 15.8 us -> 1.78 us
    unnamed x2 -> x0, waiting for transfers between devices: 423 us -> none
    psum x1 -> x0, blocking collectives: 133 us -> none  [shards(): grad_os = lax.psum(grad_share, 'dp').astype(jnp.float32)]
    pallas_call x0 -> x1, Pallas kernels: none -> 43.1 us  [reduce_grad(): pl.pallas_call(reduce_kernel, out_shape=jax.ShapeDtypeStruct((18, 1152),...]
  transfers between devices with their start and end apart: 3 -> 2, of which waited for: 3 -> 2; matrix products, arithmetic and copies ran while one was open for 1% -> 3% of each run, Pallas kernels for 0% -> 0%
where the time goes in v2:
time: 225 us; the launch traced here: 224 us
  Pallas kernels  116 us (52%)
  waiting for transfers between devices  34 us (15%)
  matrix products  30.7 us (14%)
  local copies, waits for them, and re-layouts  23.7 us (11%)
  starting transfers between devices  12.3 us (5%)
  other arithmetic  4.85 us (2%)
    pallas_call x1, Pallas kernels, gather_weights(): pl.pallas_call(gather_kernel, out_shape=[jax.ShapeDtypeStruct((4, rows *...  73.3 us
    pallas_call x1, Pallas kernels, reduce_grad(): pl.pallas_call(reduce_kernel, out_shape=jax.ShapeDtypeStruct((18, 1152),...  43.1 us
    all_to_all x1, waiting for transfers between devices, shards(): lax.all_to_all(after.reshape(frame_count, patch_count, model_width), 'seq...  18.1 us
    all_to_all x1, waiting for transfers between devices, shards(): lax.all_to_all(patch_grad, 'seq', split_axis=0, concat_axis=1, tiled=True)  15.8 us
    unnamed x47, local copies, waits for them, and re-layouts  8.43 us
    dot_general x4, matrix products, times_transposed(): lax.dot_general(left, right, (((1,), (1,)), ((), ())), preferred_element_...  8.2 us
    all_to_all x1, starting transfers between devices, shards(): lax.all_to_all(after.reshape(frame_count, patch_count, model_width), 'seq...  6.92 us
    all_to_all x1, starting transfers between devices, shards(): lax.all_to_all(patch_grad, 'seq', split_axis=0, concat_axis=1, tiled=True)  5.39 us
  transfers between devices with their start and end apart: 2, of which 2 were waited for; matrix products, arithmetic and copies ran while one was open for 3% of the time, Pallas kernels for 0%

profile of v2, /device:TPU:1, one launch (start us, length us, event | category | flops | bytes accessed | tf_op | source)
XLA Modules:
  0.0 223.8 jit_solution(11424754671322139950)
XLA Ops:
  1.9 1.7 fusion.41
  3.6 2.1 fusion.42
  6.9 73.3 %gather_weights.1 = (bf16[4,144,1152]{2,1,0:T(8,128)(2,1)S(1)}, bf16[4,288,576]{2,1,0:T(8,128)(2,1)S(1)}, bf16[4,144,1152]{2,1,0:T(8,128)(2,1)S(1)}, bf16[4,288,1728]{2,1,0:T(8,128)(2,1)}) custom-call(bf16[18,1152]{1,0:T(8,128)(2,1)S(1)} %copy-done.3, bf16[36,576]{1,0:T(8,128)(2,1)S(1)} %copy-done.5, bf16[18,1152]{1,0:T(8,128)(2,1)S(1)} %copy-done.4, ...), custom_call_target="tpu_custom_call" | custom-call | tf_op jit(solution)/shard_map/gather_weights/pallas_call | solution.py:188
  82.8 1.5 convolution_convert_fusion.5
  84.3 1.8 fusion.6
  87.0 3.1 %reduce.12 = bf16[128,1152]{1,0:T(8,128)(2,1)} reduce(bf16[128,1,1152]{2,1,0:T(2,128)(2,1)S(1)} %bitcast.210, bf16[]{:T(256)} %broadcast.92), dimensions={1}, to_apply=%bitcast.197.reduce_sub_computation | reduce | bytes 589826
  90.1 1.9 reshape.211
  92.0 6.9 %all-to-all-start = ((bf16[32,2,2304]{2,1,0:T(2,128)(2,1)}), bf16[32,2,2304]{2,1,0:T(2,128)(2,1)}, u32[]{:S(2)}, u32[]{:S(2)}) async-start(bf16[32,2,2304]{2,1,0:T(2,128)(2,1)} %reshape.211), calls=%async_computation | async-start | bytes 589824 | tf_op jit(solution)/shard_map/all_to_all | solution.py:482
  98.9 1.9 reshape.203
  100.8 18.1 %all-to-all-done = bf16[32,2,2304]{2,1,0:T(2,128)(2,1)} async-done(((bf16[32,2,2304]{2,1,0:T(2,128)(2,1)}), bf16[32,2,2304]{2,1,0:T(2,128)(2,1)}, u32[]{:S(2)}, u32[]{:S(2)}) %all-to-all-start) | async-done | bytes 294944 | tf_op jit(solution)/shard_map/all_to_all | solution.py:482
  118.9 2.3 %reshape.212 = bf16[128,1,1152]{2,1,0:T(2,128)(2,1)S(1)} reshape(bf16[32,2,2304]{2,1,0:T(2,128)(2,1)} %all-to-all-done) | data formatting | bytes 589824
  121.2 4.6 %convolution_convert_fusion.1 = bf16[128,1728]{0,1:T(8,128)(2,1)} fusion(bf16[1152,1728]{1,0:T(8,128)(2,1)} %bitcast.208, bf16[1,128,1152]{2,0,1:T(2,128)(2,1)S(1)} %bitcast.216), kind=kOutput, calls=%fused_computation.10 | convolution fusion | flops 509829120 | bytes 4718592 | tf_op jit(solution)/shard_map/dot_general | solution.py:491
  127.0 1.7 reshape_reshape.8
  128.8 2.4 %copy.92 = bf16[32,4,3,8,72]{4,0,3,1,2:T(8,128)(2,1)} copy(bf16[32,4,3,8,72]{4,3,2,1,0:T(8,128)(2,1)} %reshape_reshape.8) | data formatting | bytes 884736 | tf_op jit(solution)/shard_map/reshape;reshape | solution.py:400
  136.3 1.9 reshape.204
  138.2 4.3 %convolution_convert_fusion = bf16[128,1152]{1,0:T(8,128)(2,1)} fusion(bf16[128,1728]{1,0:T(8,128)(2,1)S(1)} %reshape.204, bf16[1152,1728]{1,0:T(8,128)(2,1)} %bitcast.209), kind=kOutput, calls=%fused_computation.9 | convolution fusion | flops 509755392 | bytes 4718592 | tf_op jit(solution)/shard_map/dot_general | solution.py:408
  142.5 1.7 reshape.205
  144.2 5.4 %all-to-all-start.1 = ((bf16[32,4,1152]{2,1,0:T(4,128)(2,1)}), bf16[32,4,1152]{2,1,0:T(4,128)(2,1)S(1)}, u32[]{:S(2)}, u32[]{:S(2)}) async-start(bf16[32,4,1152]{2,1,0:T(4,128)(2,1)} %reshape.205), calls=%async_computation.1 | async-start | bytes 589824 | tf_op jit(solution)/shard_map/all_to_all | solution.py:521
  152.0 1.7 copy.70
  153.7 15.8 %all-to-all-done.1 = bf16[32,4,1152]{2,1,0:T(4,128)(2,1)S(1)} async-done(((bf16[32,4,1152]{2,1,0:T(4,128)(2,1)}), bf16[32,4,1152]{2,1,0:T(4,128)(2,1)S(1)}, u32[]{:S(2)}, u32[]{:S(2)}) %all-to-all-start.1) | async-done | bytes 294944 | tf_op jit(solution)/shard_map/all_to_all | solution.py:521
  169.6 1.9 convolution_convert_fusion.8
  172.6 2.4 %fusion.20 = bf16[8,128,72]{1,2,0:T(8,128)(2,1)} fusion(bf16[128,8,72]{0,2,1:T(8,128)(2,1)S(1)} %bitcast.235, f32[8,128,128]{1,2,0:T(8,128)} %get-tuple-element.35, f32[8,128]{1,0:T(8,128)S(1)} %get-tuple-element.34, f32[8,128]{1,0:T(8,128)S(1)} %get-tuple-element.28, bf16[128,8,72]{0,2,1:T(8,128)(2,1)} %bitcast.240, pred[128]{0:T(512)(128)(4,1)S(1)} %copy-done.19), kind=kOutput, calls=%fused_computation.36 | convolution fusion | flops 38814848 | bytes 974976 | tf_op jit(solution)/shard_map/bhqk,bkhe->bqhe/dot_general | solution.py:434
  175.0 1.5 fusion.3.refs_1_
  179.2 43.1 %reduce_grad.1 = f32[18,1152]{1,0:T(8,128)S(1)} custom-call(bf16[576,128]{1,0:T(8,128)(2,1)S(1)} %bitcast.207, bf16[128,1152]{1,0:T(8,128)(2,1)S(1)} %fusion.3.refs_1_), custom_call_target="tpu_custom_call" | custom-call | tf_op jit(solution)/shard_map/reduce_grad/pallas_call | solution.py:387
  (71 shorter events, 18.9 us)
Async XLA Ops:
  0.6 5.7 %copy-start.11 = (bf16[1,1,128,3,576]{2,4,3,1,0:T(8,128)(2,1)S(1)}, bf16[1,1,128,3,576]{2,4,3,1,0:T(8,128)(2,1)}, u32[]{:S(2)}) copy-start(bf16[1,1,128,3,576]{2,4,3,1,0:T(8,128)(2,1)} %param.10) | copy-start | bytes 1327108
  5.7 0.6 copy-start.17
  5.7 1.1 copy-start.2
  5.7 1.1 copy-start.3
  5.7 1.1 copy-start.4
  5.7 1.1 copy-start.5
  6.3 73.9 %copy-start.9 = (bf16[1,1,128,1152]{3,2,1,0:T(8,128)(2,1)S(1)}, bf16[1,1,128,1152]{3,2,1,0:T(8,128)(2,1)}, u32[]{:S(2)}) copy-start(bf16[1,1,128,1152]{3,2,1,0:T(8,128)(2,1)} %param.9) | copy-start | bytes 884740
  80.2 1.2 copy-start
  80.7 0.9 copy-start.13
  80.7 0.9 copy-start.19
  81.4 1.4 copy-start.16
  92.0 27.0 %all-to-all-start = ((bf16[32,2,2304]{2,1,0:T(2,128)(2,1)}), bf16[32,2,2304]{2,1,0:T(2,128)(2,1)}, u32[]{:S(2)}, u32[]{:S(2)}) async-start(bf16[32,2,2304]{2,1,0:T(2,128)(2,1)} %reshape.211), calls=%async_computation | async-start | bytes 589824 | tf_op jit(solution)/shard_map/all_to_all | solution.py:482
  132.5 1.7 copy-start.8
  132.5 1.4 copy-start.6
  132.5 1.4 copy-start.10
  144.2 25.3 %all-to-all-start.1 = ((bf16[32,4,1152]{2,1,0:T(4,128)(2,1)}), bf16[32,4,1152]{2,1,0:T(4,128)(2,1)S(1)}, u32[]{:S(2)}, u32[]{:S(2)}) async-start(bf16[32,4,1152]{2,1,0:T(4,128)(2,1)} %reshape.205), calls=%async_computation.1 | async-start | bytes 589824 | tf_op jit(solution)/shard_map/all_to_all | solution.py:521
  169.6 1.9 copy-start.15
  169.6 1.9 copy-start.20
  171.5 1.1 copy-start.14
  175.0 2.1 copy-start.18
  176.5 2.7 %copy-start.1 = (bf16[128,1152]{1,0:T(8,128)(2,1)}, bf16[128,1152]{1,0:T(8,128)(2,1)S(1)}, u32[]{:S(2)}) copy-start(bf16[128,1152]{1,0:T(8,128)(2,1)S(1)} %fusion.3.refs_1_) | copy-start | bytes 884740
  176.5 1.1 copy-start.12
  177.0 1.2 copy-start.7

commit v3 on v2

v3 whole, which is shorter than its diff:
```python
import math

import jax
import jax.numpy as jnp
from jax import lax
from jax.experimental import pallas as pl
from jax.experimental.pallas import tpu as pltpu
from jax.sharding import PartitionSpec as P

HEADS = 8
HEAD = 72
SCALE = 1.0 / math.sqrt(HEAD)
MESH = pl.DeviceIdType.MESH
BF16 = jnp.bfloat16
F32 = jnp.float32
OS, QC, OC, QKV = range(4)
COLUMNS = (1152, 576, 1152, 1728)
ROWS = (18, 36, 18, 36)
CUTS = {18: (0, 48, 80, 112, 144), 36: (0, 80, 144, 224, 288)}
BLOCKS = ((OS, OC), (QC,), (QKV,))
FAR_CORE = (1, 1, 0)


def place():
    dp, seq = lax.axis_index("dp"), lax.axis_index("seq")
    return lax.rem(dp, 2), lax.div(dp, 4), lax.div(seq, 8), lax.rem(lax.div(dp, 2), 2) * 8 + lax.rem(seq, 8)


def device(core, x, y, z):
    return ((x * 2 + lax.div(z, 8)) * 2 + core, y * 8 + lax.rem(z, 8))


class Gather:
    def __init__(self, shards, landing, full, sems):
        self.shards, self.landing, self.full = shards, landing, full
        (self.zs, self.zr, self.ps, self.pr, self.ws, self.wr, self.qs, self.qr) = sems
        core, x, y, z = place()
        self.core, self.x, self.y, self.slot = core, x, y, lax.rem(z, 8)
        self.step = 1 - 2 * core
        self.next_z = device(core, x, y, lax.rem(z + self.step + 16, 16))
        self.next_y = device(core, x, lax.rem(y + self.step + 4, 4), z)
        self.next_x = device(core, lax.rem(x + self.step + 4, 4), y, z)
        self.partner = device(1 - core, x, y, z)
        self.half = lax.rem(x, 2)

    def stage(self, b):
        block = self.landing[b]
        block[self.slot] = jnp.zeros(block.shape[1:], BF16)
        at = 0
        for w in BLOCKS[b]:
            block[self.slot, at:at + ROWS[w], :] = self.shards[w][...]
            at += ROWS[w]

    def block_copy(self, b, s, slot, to, send, recv):
        block = self.landing[b].at[slot]
        return pltpu.make_async_remote_copy(
            src_ref=block, dst_ref=block, send_sem=send.at[b, s], recv_sem=recv.at[b, s],
            device_id=to, device_id_type=MESH)

    def z_copy(self, b, s, slot):
        return self.block_copy(b, s, slot, self.next_z, self.zs, self.zr)

    def pass_copy(self, b, s, slot):
        return self.block_copy(b, s, slot, self.partner, self.ps, self.pr)

    def away(self, steps):
        return lax.rem(self.slot - steps * self.step + 8, 8)

    def z_start(self, b):
        self.z_copy(b, 0, self.slot).start()

    def z_step(self, b, s):
        def go():
            slot = self.away(s + 1)
            self.z_copy(b, s, slot).wait_recv()
            if s < 2:
                self.z_copy(b, s + 1, slot).start()
            if s == 2:
                pl.when(self.core == FAR_CORE[b])(lambda: self.z_copy(b, 3, slot).start())
            self.pass_copy(b, s, slot).start()

        if s < 3:
            go()
        else:
            pl.when(self.core == FAR_CORE[b])(go)

    def z_finish(self, b):
        for s in range(3):
            self.pass_copy(b, s, lax.rem(self.slot + (s + 1) * self.step + 8, 8)).wait_recv()
        pl.when(self.core != FAR_CORE[b])(
            lambda: self.pass_copy(b, 3, lax.rem(self.slot + 4, 8)).wait_recv())

    def pack(self, w):
        b = [k for k in range(3) if w in BLOCKS[k]][0]
        at, rows = ROWS[w] * BLOCKS[b].index(w), ROWS[w]
        for k in range(8):
            self.full[w][self.y, k * rows:(k + 1) * rows, :] = self.landing[b][k, at:at + rows, :]
        self.by_half(w, self.half, lambda c: c(self.y, None, self.next_y, 0, self.ws, self.wr).start())

    def part_copy(self, w, half, share, quarter, to, s, send, recv):
        cuts = CUTS[ROWS[w]]
        first, last = (cuts[2 * half], cuts[2 * half + 2]) if share is None else (
            cuts[2 * half + share], cuts[2 * half + share + 1])
        block = self.full[w].at[quarter, pl.ds(first, last - first)]
        return pltpu.make_async_remote_copy(
            src_ref=block, dst_ref=block, send_sem=send.at[w, s], recv_sem=recv.at[w, s],
            device_id=to, device_id_type=MESH)

    def by_half(self, w, half, go):
        for h in range(2):
            @pl.when(half == h)
            def _():
                go(lambda quarter, share, to, s, send, recv: self.part_copy(
                    w, h, share, quarter, to, s, send, recv))

    def by_share(self, w, half, share, go):
        for c in range(2):
            @pl.when(share == c)
            def _():
                self.by_half(w, half, lambda copy: go(lambda quarter, to, s, send, recv: copy(
                    quarter, c, to, s, send, recv)))

    def near(self):
        return lax.rem(self.y - self.step + 4, 4)

    def far(self):
        return lax.rem(self.y + 2, 4)

    def y_step(self, w):
        def near(copy):
            copy(self.near(), None, self.next_y, 0, self.ws, self.wr).wait_recv()
            copy(self.near(), None, self.next_x, 2, self.ws, self.wr).start()
            copy(self.near(), None, self.partner, 0, self.qs, self.qr).start()

        self.by_half(w, self.half, near)
        self.by_share(w, self.half, self.core, lambda copy: copy(
            self.near(), self.next_y, 1, self.ws, self.wr).start())

    def y_last(self, w):
        def far(copy):
            copy(self.far(), self.next_y, 1, self.ws, self.wr).wait_recv()
            copy(self.far(), self.next_x, 3, self.ws, self.wr).start()
            copy(self.far(), self.partner, 1, self.qs, self.qr).start()

        self.by_share(w, self.half, self.core, far)

    def x_step(self, w):
        def near(copy):
            copy(self.near(), None, self.next_x, 2, self.ws, self.wr).wait_recv()
            copy(self.near(), None, self.partner, 2, self.qs, self.qr).start()

        self.by_half(w, 1 - self.half, near)

    def x_last(self, w):
        def far(copy):
            copy(self.far(), self.next_x, 3, self.ws, self.wr).wait_recv()
            copy(self.far(), self.partner, 3, self.qs, self.qr).start()

        self.by_share(w, 1 - self.half, self.core, far)

    def finish(self, w):
        other = lax.rem(self.y + self.step + 4, 4)
        self.by_half(w, self.half, lambda copy: copy(
            other, None, self.partner, 0, self.qs, self.qr).wait_recv())
        self.by_half(w, 1 - self.half, lambda copy: copy(
            other, None, self.partner, 2, self.qs, self.qr).wait_recv())
        self.by_share(w, self.half, 1 - self.core, lambda copy: copy(
            self.far(), self.partner, 1, self.qs, self.qr).wait_recv())
        self.by_share(w, 1 - self.half, 1 - self.core, lambda copy: copy(
            self.far(), self.partner, 3, self.qs, self.qr).wait_recv())

    def drain(self):
        for b in range(3):
            for s in range(3):
                self.z_copy(b, s, self.away(s)).wait_send()
                self.pass_copy(b, s, self.away(s + 1)).wait_send()

            @pl.when(self.core == FAR_CORE[b])
            def _():
                self.z_copy(b, 3, self.away(3)).wait_send()
                self.pass_copy(b, 3, self.away(4)).wait_send()

        for w in range(4):
            def mine(copy):
                copy(self.y, None, self.next_y, 0, self.ws, self.wr).wait_send()
                copy(self.near(), None, self.next_x, 2, self.ws, self.wr).wait_send()
                copy(self.near(), None, self.partner, 0, self.qs, self.qr).wait_send()

            def mine_far(copy):
                copy(self.near(), self.next_y, 1, self.ws, self.wr).wait_send()
                copy(self.far(), self.next_x, 3, self.ws, self.wr).wait_send()
                copy(self.far(), self.partner, 1, self.qs, self.qr).wait_send()

            self.by_half(w, self.half, mine)
            self.by_half(w, 1 - self.half, lambda copy: copy(
                self.near(), None, self.partner, 2, self.qs, self.qr).wait_send())
            self.by_share(w, self.half, self.core, mine_far)
            self.by_share(w, 1 - self.half, self.core, lambda copy: copy(
                self.far(), self.partner, 3, self.qs, self.qr).wait_send())


class Switch:
    def __init__(self, out, taken, send, recv):
        self.out, self.taken, self.send, self.recv = out, taken, send, recv
        self.dp, self.seq = lax.axis_index("dp"), lax.axis_index("seq")

    def copy(self, k):
        to = lax.rem(self.seq + k, 32)
        return pltpu.make_async_remote_copy(
            src_ref=self.out.at[to], dst_ref=self.taken.at[self.seq],
            send_sem=self.send.at[k], recv_sem=self.recv.at[k],
            device_id=(self.dp, to), device_id_type=MESH)

    def start(self):
        @pl.loop(1, 32)
        def _(k):
            self.copy(k).start()

        self.taken[self.seq] = self.out[self.seq]

    def wait(self):
        @pl.loop(1, 32)
        def _(k):
            block = self.taken.at[lax.rem(self.seq - k + 32, 32)]
            pltpu.make_async_remote_copy(
                src_ref=block, dst_ref=block, send_sem=self.send.at[k], recv_sem=self.recv.at[k],
                device_id=(self.dp, lax.rem(self.seq + k, 32)), device_id_type=MESH).wait_recv()

    def drain(self):
        @pl.loop(1, 32)
        def _(k):
            self.copy(k).wait_send()


class Reduce:
    def __init__(self, partial, taken, pieces, plane, total, z_out, z_in, x_out, x_in, sems):
        self.partial, self.taken, self.pieces, self.plane = partial, taken, pieces, plane
        self.total, self.z_out, self.z_in, self.x_out, self.x_in = total, z_out, z_in, x_out, x_in
        (self.cs, self.cr, self.ps, self.pr, self.zs, self.zr, self.xs, self.xr) = sems
        self.core, self.x, self.y, self.z = place()
        self.holds = jnp.logical_and(self.x < 3, lax.div(self.y, 2) == self.core)
        self.me = self.x * 4 + self.y

    def greet(self, barrier):
        def signal(d):
            pl.semaphore_signal(barrier, inc=1, device_id=d, device_id_type=MESH)

        core, x, y, z = self.core, self.x, self.y, self.z

        @pl.loop(1, 16)
        def _(k):
            signal(device(core, lax.rem(x + lax.div(k, 4), 4), lax.rem(y + lax.rem(k, 4), 4), z))
            signal(device(core, x, y, lax.rem(z + k, 16)))

        @pl.loop(0, 4)
        def _(k):
            signal(device(1 - core, lax.rem(x + k, 4), y, z))

        return 34

    def core_copy(self):
        return pltpu.make_async_remote_copy(
            src_ref=self.partial.at[1 - self.core], dst_ref=self.taken, send_sem=self.cs, recv_sem=self.cr,
            device_id=device(1 - self.core, self.x, self.y, self.z), device_id_type=MESH)

    def plane_copy(self, upper, x):
        return pltpu.make_async_remote_copy(
            src_ref=self.pieces.at[upper, x], dst_ref=self.plane.at[self.me],
            send_sem=self.ps.at[upper * 3 + x], recv_sem=self.pr.at[self.me],
            device_id=device(self.core, x, self.core * 2 + upper, self.z), device_id_type=MESH)

    def is_me(self, upper, x):
        return jnp.logical_and(self.x == x, self.y == self.core * 2 + upper)

    def plane_start(self):
        self.core_copy().wait_recv()
        for upper in range(2):
            for x in range(3):
                rows, columns = slice(144 * upper, 144 * upper + 144), slice(384 * x, 384 * x + 384)
                self.pieces[upper, x] = (
                    self.partial[self.core, rows, columns].astype(F32)
                    + self.taken[rows, columns].astype(F32)).astype(BF16)
        for upper in range(2):
            for x in range(3):
                pl.when(jnp.logical_not(self.is_me(upper, x)))(
                    lambda: self.plane_copy(upper, x).start())

                @pl.when(self.is_me(upper, x))
                def _():
                    self.plane[self.me] = self.pieces[upper, x]

    def z_copy(self, k):
        to = lax.rem(self.z + k, 16)
        return pltpu.make_async_remote_copy(
            src_ref=self.z_out.at[lax.rem(to, 8)], dst_ref=self.z_in.at[self.z],
            send_sem=self.zs.at[k], recv_sem=self.zr.at[self.z],
            device_id=device(self.core, self.x, self.y, to), device_id_type=MESH)

    def z_start(self):
        @pl.when(self.holds)
        def _():
            @pl.loop(0, 16)
            def _(k):
                @pl.when(k != self.me)
                def _():
                    block = self.plane.at[k]
                    pltpu.make_async_remote_copy(
                        src_ref=block, dst_ref=block, send_sem=self.ps.at[0], recv_sem=self.pr.at[k],
                        device_id=device(1 - self.core, self.x, self.y, self.z), device_id_type=MESH).wait_recv()

            for r in range(3):
                rows = slice(48 * r, 48 * r + 48)
                sum_rows = self.plane[0, rows].astype(F32)
                for k in range(1, 16):
                    sum_rows = sum_rows + self.plane[k, rows].astype(F32)
                self.total[rows] = sum_rows
            self.z_out[...] = jnp.zeros(self.z_out.shape, BF16)
            for k in range(8):
                self.z_out[k, 0:18, :] = self.total[18 * k:18 * k + 18, :].astype(BF16)

            @pl.loop(1, 16)
            def _(k):
                self.z_copy(k).start()

            self.z_in[self.z] = self.z_out[lax.rem(self.z, 8)]

    def x_copy(self, k):
        other = lax.div(k, 4)
        return pltpu.make_async_remote_copy(
            src_ref=self.x_out, dst_ref=self.x_in.at[self.x],
            send_sem=self.xs.at[k], recv_sem=self.xr.at[self.x],
            device_id=device(lax.rem(self.core + other, 2), lax.rem(self.x + k, 4), self.y, self.z),
            device_id_type=MESH)

    def x_start(self):
        @pl.when(self.holds)
        def _():
            @pl.loop(0, 16)
            def _(k):
                @pl.when(k != self.z)
                def _():
                    block = self.z_in.at[k]
                    pltpu.make_async_remote_copy(
                        src_ref=block, dst_ref=block, send_sem=self.zs.at[0], recv_sem=self.zr.at[k],
                        device_id=device(1 - self.core, self.x, self.y, self.z), device_id_type=MESH).wait_recv()

            sum_rows = self.z_in[0].astype(F32)
            for k in range(1, 16):
                sum_rows = sum_rows + self.z_in[k].astype(F32)
            self.x_out[...] = sum_rows.astype(BF16)

            @pl.loop(1, 8)
            def _(k):
                self.x_copy(k).start()

            self.x_in[self.x] = self.x_out[...]

    def finish(self, out):
        for k in range(3):
            @pl.when(jnp.logical_not(jnp.logical_and(self.holds, self.x == k)))
            def _():
                block = self.x_in.at[k]
                pltpu.make_async_remote_copy(
                    src_ref=block, dst_ref=block, send_sem=self.xs.at[0], recv_sem=self.xr.at[k],
                    device_id=device(1 - self.core, self.x, self.y, self.z), device_id_type=MESH).wait_recv()
            out[:, 384 * k:384 * k + 384] = self.x_in[k, 0:18, :].astype(F32)

    def drain(self):
        self.core_copy().wait_send()
        for upper in range(2):
            for x in range(3):
                pl.when(jnp.logical_not(self.is_me(upper, x)))(
                    lambda: self.plane_copy(upper, x).wait_send())

        @pl.when(self.holds)
        def _():
            @pl.loop(1, 16)
            def _(k):
                self.z_copy(k).wait_send()

            @pl.loop(1, 8)
            def _(k):
                self.x_copy(k).wait_send()


REDUCE_SCRATCH = [
    pltpu.VMEM((2, 288, 1152), BF16),
    pltpu.VMEM((288, 1152), BF16),
    pltpu.VMEM((2, 3, 144, 384), BF16),
    pltpu.VMEM((16, 144, 384), BF16),
    pltpu.VMEM((144, 384), F32),
    pltpu.VMEM((8, 32, 384), BF16),
    pltpu.VMEM((16, 32, 384), BF16),
    pltpu.VMEM((32, 384), BF16),
    pltpu.VMEM((3, 32, 384), BF16),
]
REDUCE_SEMS = [pltpu.SemaphoreType.DMA, pltpu.SemaphoreType.DMA] + [
    pltpu.SemaphoreType.DMA((n,)) for n in (6, 16, 16, 16, 8, 3)]


def times(left, right):
    return jnp.dot(left, right, preferred_element_type=F32)


def times_transposed(left, right):
    return lax.dot_general(left, right, (((1,), (1,)), ((), ())), preferred_element_type=F32)


def transposed_times(left, right):
    return lax.dot_general(left, right, (((0,), (0,)), ((), ())), preferred_element_type=F32)


def split_heads(ref, array):
    for h in range(HEADS):
        ref[h] = array[HEAD * h:HEAD * h + HEAD, :]


def attend(head, queries, keys, values, visible, weights, out):
    scores = transposed_times(keys[head], queries[head]) * SCALE
    if visible is not None:
        scores = jnp.where(visible, scores, -1e30)
    powers = jnp.exp(scores - jnp.max(scores, axis=0, keepdims=True))
    share = powers / jnp.sum(powers, axis=0, keepdims=True)
    weights[head] = share
    out[head] = times(values[head], share.astype(BF16)).astype(BF16)


def attend_grad(head, upstream, queries, keys, values, weights, query_grad, key_grad, value_grad):
    upper, share = upstream[head], weights[head]
    share_grad = transposed_times(values[head], upper)
    score_grad = (share * (share_grad - jnp.sum(share_grad * share, axis=0, keepdims=True))).astype(BF16)
    query_grad[head] = (SCALE * times(keys[head], score_grad)).astype(BF16)
    if key_grad is not None:
        value_grad[head] = times_transposed(upper, share.astype(BF16)).astype(BF16)
        key_grad[head] = (SCALE * times_transposed(queries[head], score_grad)).astype(BF16)


def each_head(go):
    @pl.loop(0, HEADS // 2)
    def _(pair):
        go(2 * pair)
        go(2 * pair + 1)


def block_pair(
    tokens, qkv, text, length, w_os, w_qc, w_oc, w_qkv, cotangent,
    heads_out, tokens_grad, qkv_grad, os_grad,
    full_os, full_qc, full_oc, full_qkv, land_pair, land_qc, land_qkv,
    gz_send, gz_recv, gp_send, gp_recv, gw_send, gw_recv, gq_send, gq_recv,
    to_patches, from_frames, to_frames, from_patches, s1_send, s1_recv, s2_send, s2_recv,
    spatial_w, cross_w, temporal_w, mixed_heads, mixed_t, cross_queries, cross_heads, temporal, upstream,
    temporal_heads, temporal_grads, wide_t, hidden_ref, *reduce_refs,
):
    full = (full_os, full_qc, full_oc, full_qkv)
    g = Gather((w_os, w_qc, w_oc, w_qkv), (land_pair, land_qc, land_qkv), full,
               (gz_send, gz_recv, gp_send, gp_recv, gw_send, gw_recv, gq_send, gq_recv))
    forth = Switch(to_patches, from_frames, s1_send, s1_recv)
    back = Switch(to_frames, from_patches, s2_send, s2_recv)
    r = Reduce(*reduce_refs[0:9], reduce_refs[9:17])

    barrier = pltpu.get_barrier_semaphore()
    greeted = r.greet(barrier)
    core, x, y, z = place()

    @pl.loop(0, 21)
    def _(k):
        to = device(core, x, lax.rem(y + 1 + lax.div(k, 7), 4),
                    lax.div(z, 8) * 8 + lax.rem(z + 1 + lax.rem(k, 7), 8))
        pl.semaphore_signal(barrier, inc=1, device_id=to, device_id_type=MESH)

    for b in range(3):
        g.stage(b)
    pl.semaphore_wait(barrier, greeted + 21)

    def whole(w):
        return full[w][...].reshape(-1, COLUMNS[w])

    def join(heads, groups=1):
        for i in range(groups):
            for h in range(HEADS):
                at = (i * HEADS + h) * HEAD
                wide_t[at:at + HEAD, :] = heads[i, h] if groups > 1 else heads[h]
        return wide_t[0:groups * HEADS * HEAD, :].T

    g.z_start(0)
    g.z_start(1)
    for s in range(4):
        for h in (2 * s, 2 * s + 1):
            attend(h, qkv.at[0], qkv.at[1], qkv.at[2], None, spatial_w, mixed_heads)
        g.z_step(0, s)
        g.z_step(1, s)
    g.z_start(2)
    g.z_finish(0)
    g.pack(OS)
    g.z_finish(1)
    g.pack(QC)
    g.pack(OC)
    mixed = join(mixed_heads)
    mixed_t[...] = wide_t[0:576, :]
    g.z_step(2, 0)
    g.y_step(OS)
    g.y_step(QC)
    g.y_last(OS)
    g.z_step(2, 1)
    g.x_step(OS)
    g.y_step(OC)
    g.y_last(QC)
    g.x_last(OS)
    g.x_step(QC)
    g.z_step(2, 2)
    g.finish(OS)
    hidden = (tokens[...].astype(F32) + times(mixed, whole(OS))).astype(BF16)
    hidden_ref[...] = hidden
    g.y_last(OC)
    g.x_step(OC)
    g.x_last(QC)
    g.z_step(2, 3)
    g.finish(QC)
    split_heads(cross_queries, times(hidden, whole(QC)).astype(BF16).T)
    g.x_last(OC)
    g.z_finish(2)
    g.pack(QKV)
    seen = lax.broadcasted_iota(jnp.int32, (128, 128), 0) < length[0]
    each_head(lambda h: attend(h, cross_queries, text.at[0], text.at[1], seen, cross_w, cross_heads))
    g.finish(OC)
    after = (hidden_ref[...].astype(F32) + times(join(cross_heads), whole(OC))).astype(BF16)
    to_patches[...] = after.reshape(32, 4, 1152)
    forth.start()
    g.y_step(QKV)
    split_heads(upstream, cotangent[...].reshape(128, 576).T)
    g.y_last(QKV)
    g.x_step(QKV)
    g.x_last(QKV)
    g.finish(QKV)
    forth.wait()

    projected = times(from_frames[...].reshape(128, 1152), whole(QKV)).astype(BF16).T
    for i in range(3):
        split_heads(temporal.at[i], projected[576 * i:576 * i + 576, :])
    same = (lax.rem(lax.broadcasted_iota(jnp.int32, (128, 128), 0), 4)
            == lax.rem(lax.broadcasted_iota(jnp.int32, (128, 128), 1), 4))

    def temporal_head(h):
        attend(h, temporal.at[0], temporal.at[1], temporal.at[2], same, temporal_w, temporal_heads)
        attend_grad(h, upstream, temporal.at[0], temporal.at[1], temporal.at[2], temporal_w,
                    temporal_grads.at[0], temporal_grads.at[1], temporal_grads.at[2])

    each_head(temporal_head)
    patch_grad = times_transposed(join(temporal_grads, 3), whole(QKV)).astype(BF16)
    to_frames[...] = patch_grad.reshape(32, 4, 1152)
    back.start()
    heads_out[...] = join(temporal_heads).reshape(32, 4, 576)
    g.drain()
    forth.drain()
    back.wait()

    after_grad = from_patches[...].reshape(128, 1152)
    split_heads(upstream, times_transposed(after_grad, whole(OC)).astype(BF16).T)
    each_head(lambda h: attend_grad(
        h, upstream, cross_queries, text.at[0], text.at[1], cross_w, cross_heads, None, None))
    hidden_grad = (after_grad.astype(F32) + times_transposed(join(cross_heads), whole(QC))).astype(BF16)
    tokens_grad[...] = hidden_grad
    for half in range(2):
        r.partial[half] = times(mixed_t[288 * half:288 * half + 288, :], hidden_grad).astype(BF16)
    r.core_copy().start()
    split_heads(upstream, times_transposed(hidden_grad, whole(OS)).astype(BF16).T)
    r.plane_start()
    each_head(lambda h: attend_grad(
        h, upstream, qkv.at[0], qkv.at[1], qkv.at[2], spatial_w, qkv_grad.at[0], qkv_grad.at[1],
        qkv_grad.at[2]))
    r.z_start()
    r.x_start()
    r.finish(os_grad)
    back.drain()
    r.drain()


def shards(tokens, spatial_qkv, text_kv, text_len, w_os, w_qc, w_oc, w_qkv, cotangent):
    heads = (HEADS, HEAD, 128)
    vmem = pl.BlockSpec(memory_space=pltpu.VMEM)
    dma = pltpu.SemaphoreType.DMA
    slabs = pltpu.VMEM((32, 4, 1152), BF16)
    temporal_heads, tokens_grad, qkv_grad, os_grad = pl.pallas_call(
        block_pair,
        out_shape=[
            jax.ShapeDtypeStruct((32, 4, 576), BF16),
            jax.ShapeDtypeStruct((128, 1152), BF16),
            jax.ShapeDtypeStruct((3,) + heads, BF16),
            jax.ShapeDtypeStruct((18, 1152), F32),
        ],
        in_specs=[vmem] * 3 + [pl.BlockSpec(memory_space=pltpu.SMEM)] + [vmem] * 5,
        out_specs=[vmem] * 4,
        scratch_shapes=[pltpu.VMEM((4, 8 * rows, columns), BF16) for rows, columns in zip(ROWS, COLUMNS)]
        + [pltpu.VMEM((8, 48, columns), BF16) for columns in (1152, 576, 1728)]
        + [dma((3, 4))] * 4 + [dma((4, 4))] * 4
        + [slabs] * 4 + [dma((32,))] * 4
        + [pltpu.VMEM((HEADS, 128, 128), F32)] * 3
        + [pltpu.VMEM(heads, BF16), pltpu.VMEM((576, 128), BF16), pltpu.VMEM(heads, BF16), pltpu.VMEM(heads, BF16),
           pltpu.VMEM((3,) + heads, BF16), pltpu.VMEM(heads, BF16), pltpu.VMEM(heads, BF16),
           pltpu.VMEM((3,) + heads, BF16), pltpu.VMEM((1728, 128), BF16), pltpu.VMEM((128, 1152), BF16)]
        + REDUCE_SCRATCH + REDUCE_SEMS,
        compiler_params=pltpu.CompilerParams(
            collective_id=0, has_side_effects=True, vmem_limit_bytes=56 * 2**20),
        name="block_pair",
    )(
        tokens.reshape(128, 1152),
        jnp.transpose(spatial_qkv[0, 0], (1, 2, 0)).reshape((3,) + heads),
        jnp.transpose(text_kv[0], (1, 2, 0)).reshape((2,) + heads),
        text_len, w_os, w_qc, w_oc, w_qkv,
        cotangent.reshape(32, 4, 576),
    )
    return (
        temporal_heads[None],
        tokens_grad[None, None],
        jnp.transpose(qkv_grad.reshape(3, 576, 128), (2, 0, 1))[None, None],
        os_grad,
    )


def solution(mesh):
    placed = (
        P("dp", "seq", None, None),
        P("dp", "seq", None, None, None),
        P("dp", None, None, None),
        P("dp"),
        P("seq", None),
        P("seq", None),
        P("seq", None),
        P("seq", None),
        P("dp", None, "seq", None),
    )
    return jax.shard_map(
        shards,
        mesh=mesh,
        in_specs=placed,
        out_specs=(
            P("dp", None, "seq", None),
            P("dp", "seq", None, None),
            P("dp", "seq", None, None, None),
            P("seq", None),
        ),
        check_vma=False,
    )
```

time: 225 us -> 145 us (0.64)
  waiting for transfers between devices: 34 us -> 0 us
  matrix products: 30.7 us -> 0 us
  Pallas kernels: 116 us -> 139 us
  local copies, waits for them, and re-layouts: 23.7 us -> 4.06 us
  starting transfers between devices: 12.3 us -> 0 us
  other arithmetic: 4.85 us -> 0 us
    all_to_all x2 -> x0, waiting for transfers between devices: 34 us -> none  [the longest x1 18.1 us: shards(): lax.all_to_all(after.reshape(frame_count, patch_count, model_width), 'seq...]
    dot_general x21 -> x0, matrix products: 26.1 us -> none  [the longest x4 8.2 us: times_transposed(): lax.dot_general(left, right, (((1,), (1,)), ((), ())), preferred_element_...]
    pallas_call x2 -> x1, Pallas kernels: 116 us -> 139 us  [shards(): pl.pallas_call(block_pair, out_shape=[jax.ShapeDtypeStruct((32, 4, 576),...]
    all_to_all x2 -> x0, starting transfers between devices: 12.3 us -> none  [the longest x1 6.92 us: shards(): lax.all_to_all(after.reshape(frame_count, patch_count, model_width), 'seq...]
    reshape x6 -> x0, local copies, waits for them, and re-layouts: 6.91 us -> none  [the longest x1 1.91 us: split_heads(): return array.reshape(array.shape[:-1] + (HEADS, HEAD))]
    sub x3 -> x0, matrix products: 4.64 us -> none  [attend(): weights = jax.nn.softmax(scores, axis=-1)]
    unnamed x47 -> x10, local copies, waits for them, and re-layouts: 8.43 us -> 4.06 us
    another operation x2 -> x0, local copies, waits for them, and re-layouts: 4.12 us -> none  [split_heads(): return array.reshape(array.shape[:-1] + (HEADS, HEAD))]
  transfers between devices with their start and end apart: 2 -> 0, of which waited for: 2 -> 0; matrix products, arithmetic and copies ran while one was open for 3% -> 0% of each run, Pallas kernels for 0% -> 0%
where the time goes in v3:
time: 145 us; the launch traced here: 144 us
  Pallas kernels  139 us (96%)
  local copies, waits for them, and re-layouts  4.06 us (3%)
    pallas_call x1, Pallas kernels, shards(): pl.pallas_call(block_pair, out_shape=[jax.ShapeDtypeStruct((32, 4, 576),...  139 us
    unnamed x10, local copies, waits for them, and re-layouts  4.06 us

profile of v3, /device:TPU:1, one launch (start us, length us, event | category | flops | bytes accessed | tf_op | source)
XLA Modules:
  0.0 144.4 jit_solution(12217529106398718155)
XLA Ops:
  1.3 139.0 %block_pair.1 = (bf16[32,4,576]{2,1,0:T(4,128)(2,1)}, bf16[128,1152]{1,0:T(8,128)(2,1)}, bf16[3,8,72,128]{3,2,1,0:T(8,128)(2,1)}, f32[18,1152]{1,0:T(8,128)}) custom-call(bf16[128,1152]{1,0:T(8,128)(2,1)} %bitcast.22, bf16[3,8,72,128]{3,2,1,0:T(8,128)(2,1)} %bitcast.19, bf16[2,8,72,128]{3,2,1,0:T(8,128)(2,1)} %bitcast.23, s32[1]{0:T(128)S(6)} %copy.17.length, ...), custom_call_target="tpu_custom_call" | custom-call | tf_op jit(solution)/shard_map/block_pair/pallas_call | solution.py:583
  140.3 0.0 copy-start.1
  140.3 0.0 copy-start
  140.3 1.7 %copy.18 = bf16[1,32,4,576]{3,2,1,0:T(4,128)(2,1)} copy(bf16[1,32,4,576]{3,2,1,0:T(4,128)(2,1)} %bitcast.24) | data formatting | bytes 294912
  142.0 0.0 copy-done.1
  142.0 0.7 copy.19
  142.7 0.0 copy-done
  142.7 0.0 copy-start.2
  142.7 0.8 copy.20
  143.5 0.2 copy-done.2
  143.7 0.6 copy.21
Async XLA Ops:
  140.3 1.7 %copy-start.1 = (bf16[128,1152]{1,0:T(8,128)(2,1)S(1)}, bf16[128,1152]{1,0:T(8,128)(2,1)}, u32[]{:S(2)}) copy-start(bf16[128,1152]{1,0:T(8,128)(2,1)} %get-tuple-element.9) | copy-start | bytes 884740
  140.3 2.4 %copy-start = (bf16[3,8,72,128]{3,2,1,0:T(8,128)(2,1)S(1)}, bf16[3,8,72,128]{3,2,1,0:T(8,128)(2,1)}, u32[]{:S(2)}) copy-start(bf16[3,8,72,128]{3,2,1,0:T(8,128)(2,1)} %get-tuple-element.10) | copy-start | bytes 1327108
  142.7 1.0 copy-start.2

commit v4 on v3

v4 whole, which is shorter than its diff:
```python
import math

import jax
import jax.numpy as jnp
from jax import lax
from jax.experimental import pallas as pl
from jax.experimental.pallas import tpu as pltpu
from jax.sharding import PartitionSpec as P

HEADS = 8
HEAD = 72
SCALE = 1.0 / math.sqrt(HEAD)
MESH = pl.DeviceIdType.MESH
BF16 = jnp.bfloat16
F32 = jnp.float32
OS, QC, OC, TQ, TK, TV = WEIGHTS = range(6)
COLUMNS = (1152, 576, 1152, 576, 576, 576)
ROWS = (18, 36, 18, 36, 36, 36)
CUTS = {18: (0, 48, 80, 112, 144), 36: (0, 80, 144, 224, 288)}
FAR_CORE = (1, 1, 1, 0, 0, 0)


def place():
    dp, seq = lax.axis_index("dp"), lax.axis_index("seq")
    return lax.rem(dp, 2), lax.div(dp, 4), lax.div(seq, 8), lax.rem(lax.div(dp, 2), 2) * 8 + lax.rem(seq, 8)


def device(core, x, y, z):
    return ((x * 2 + lax.div(z, 8)) * 2 + core, y * 8 + lax.rem(z, 8))


def greet(barrier):
    core, x, y, z = place()

    def signal(*to):
        pl.semaphore_signal(barrier, inc=1, device_id=device(*to), device_id_type=MESH)

    @pl.loop(1, 16)
    def _(k):
        signal(core, x, y, lax.rem(z + k, 16))

    @pl.loop(0, 4)
    def _(k):
        signal(1 - core, lax.rem(x + k, 4), y, z)

    for k in range(1, 4):
        side = lax.rem(y + k, 4)

        @pl.loop(0, 8)
        def _(j):
            signal(core, x, side, lax.div(z, 8) * 8 + j)

        for j in range(4):
            if j:
                signal(core, lax.rem(x + j, 4), side, z)
        signal(core, lax.rem(x + k, 4), y, z)
    return 55


class Gather:
    def __init__(self, shards, landing, full, sems):
        self.shards, self.landing, self.full = shards, landing, full
        (self.zs, self.zr, self.ps, self.pr, self.ws, self.wr, self.qs, self.qr) = sems
        core, x, y, z = place()
        self.core, self.x, self.y, self.slot = core, x, y, lax.rem(z, 8)
        self.step = 1 - 2 * core
        self.next_z = device(core, x, y, lax.rem(z + self.step + 16, 16))
        self.next_y = device(core, x, lax.rem(y + self.step + 4, 4), z)
        self.next_x = device(core, lax.rem(x + self.step + 4, 4), y, z)
        self.partner = device(1 - core, x, y, z)
        self.half = lax.rem(x, 2)

    def stage(self, b):
        shard = self.shards[min(b, TQ)]
        first = 576 * max(b - TQ, 0)
        self.landing[b][self.slot] = shard[:, first:first + COLUMNS[b]]

    def block_copy(self, b, s, slot, to, send, recv):
        block = self.landing[b].at[slot]
        return pltpu.make_async_remote_copy(
            src_ref=block, dst_ref=block, send_sem=send.at[b, s], recv_sem=recv.at[b, s],
            device_id=to, device_id_type=MESH)

    def z_copy(self, b, s, slot):
        return self.block_copy(b, s, slot, self.next_z, self.zs, self.zr)

    def pass_copy(self, b, s, slot):
        return self.block_copy(b, s, slot, self.partner, self.ps, self.pr)

    def away(self, steps):
        return lax.rem(self.slot - steps * self.step + 8, 8)

    def z_start(self, b):
        self.z_copy(b, 0, self.slot).start()

    def z_step(self, b, s):
        def go():
            slot = self.away(s + 1)
            self.z_copy(b, s, slot).wait_recv()
            if s < 2:
                self.z_copy(b, s + 1, slot).start()
            if s == 2:
                pl.when(self.core == FAR_CORE[b])(lambda: self.z_copy(b, 3, slot).start())
            self.pass_copy(b, s, slot).start()

        if s < 3:
            go()
        else:
            pl.when(self.core == FAR_CORE[b])(go)

    def z_finish(self, b):
        for s in range(3):
            self.pass_copy(b, s, lax.rem(self.slot + (s + 1) * self.step + 8, 8)).wait_recv()
        pl.when(self.core != FAR_CORE[b])(
            lambda: self.pass_copy(b, 3, lax.rem(self.slot + 4, 8)).wait_recv())

    def pack(self, w):
        rows = ROWS[w]
        for k in range(8):
            self.full[w][self.y, k * rows:(k + 1) * rows, :] = self.landing[w][k]
        self.by_half(w, self.half, lambda c: c(self.y, None, self.next_y, 0, self.ws, self.wr).start())

    def part_copy(self, w, half, share, quarter, to, s, send, recv):
        cuts = CUTS[ROWS[w]]
        first, last = (cuts[2 * half], cuts[2 * half + 2]) if share is None else (
            cuts[2 * half + share], cuts[2 * half + share + 1])
        block = self.full[w].at[quarter, pl.ds(first, last - first)]
        return pltpu.make_async_remote_copy(
            src_ref=block, dst_ref=block, send_sem=send.at[w, s], recv_sem=recv.at[w, s],
            device_id=to, device_id_type=MESH)

    def by_half(self, w, half, go):
        for h in range(2):
            @pl.when(half == h)
            def _():
                go(lambda quarter, share, to, s, send, recv: self.part_copy(
                    w, h, share, quarter, to, s, send, recv))

    def by_share(self, w, half, share, go):
        for c in range(2):
            @pl.when(share == c)
            def _():
                self.by_half(w, half, lambda copy: go(lambda quarter, to, s, send, recv: copy(
                    quarter, c, to, s, send, recv)))

    def near(self):
        return lax.rem(self.y - self.step + 4, 4)

    def far(self):
        return lax.rem(self.y + 2, 4)

    def y_step(self, w):
        def near(copy):
            copy(self.near(), None, self.next_y, 0, self.ws, self.wr).wait_recv()
            copy(self.near(), None, self.next_x, 2, self.ws, self.wr).start()
            copy(self.near(), None, self.partner, 0, self.qs, self.qr).start()

        self.by_half(w, self.half, near)
        self.by_share(w, self.half, self.core, lambda copy: copy(
            self.near(), self.next_y, 1, self.ws, self.wr).start())

    def y_last(self, w):
        def far(copy):
            copy(self.far(), self.next_y, 1, self.ws, self.wr).wait_recv()
            copy(self.far(), self.next_x, 3, self.ws, self.wr).start()
            copy(self.far(), self.partner, 1, self.qs, self.qr).start()

        self.by_share(w, self.half, self.core, far)

    def x_step(self, w):
        def near(copy):
            copy(self.near(), None, self.next_x, 2, self.ws, self.wr).wait_recv()
            copy(self.near(), None, self.partner, 2, self.qs, self.qr).start()

        self.by_half(w, 1 - self.half, near)

    def x_last(self, w):
        def far(copy):
            copy(self.far(), self.next_x, 3, self.ws, self.wr).wait_recv()
            copy(self.far(), self.partner, 3, self.qs, self.qr).start()

        self.by_share(w, 1 - self.half, self.core, far)

    def finish(self, w):
        other = lax.rem(self.y + self.step + 4, 4)
        self.by_half(w, self.half, lambda copy: copy(
            other, None, self.partner, 0, self.qs, self.qr).wait_recv())
        self.by_half(w, 1 - self.half, lambda copy: copy(
            other, None, self.partner, 2, self.qs, self.qr).wait_recv())
        self.by_share(w, self.half, 1 - self.core, lambda copy: copy(
            self.far(), self.partner, 1, self.qs, self.qr).wait_recv())
        self.by_share(w, 1 - self.half, 1 - self.core, lambda copy: copy(
            self.far(), self.partner, 3, self.qs, self.qr).wait_recv())

    def drain(self):
        for b in WEIGHTS:
            for s in range(3):
                self.z_copy(b, s, self.away(s)).wait_send()
                self.pass_copy(b, s, self.away(s + 1)).wait_send()

            @pl.when(self.core == FAR_CORE[b])
            def _():
                self.z_copy(b, 3, self.away(3)).wait_send()
                self.pass_copy(b, 3, self.away(4)).wait_send()

        for w in WEIGHTS:
            def mine(copy):
                copy(self.y, None, self.next_y, 0, self.ws, self.wr).wait_send()
                copy(self.near(), None, self.next_x, 2, self.ws, self.wr).wait_send()
                copy(self.near(), None, self.partner, 0, self.qs, self.qr).wait_send()

            def mine_far(copy):
                copy(self.near(), self.next_y, 1, self.ws, self.wr).wait_send()
                copy(self.far(), self.next_x, 3, self.ws, self.wr).wait_send()
                copy(self.far(), self.partner, 1, self.qs, self.qr).wait_send()

            self.by_half(w, self.half, mine)
            self.by_half(w, 1 - self.half, lambda copy: copy(
                self.near(), None, self.partner, 2, self.qs, self.qr).wait_send())
            self.by_share(w, self.half, self.core, mine_far)
            self.by_share(w, 1 - self.half, self.core, lambda copy: copy(
                self.far(), self.partner, 3, self.qs, self.qr).wait_send())


class Switch:
    def __init__(self, out, taken, send, recv):
        self.out, self.taken, self.send, self.recv = out, taken, send, recv
        self.dp, self.seq = lax.axis_index("dp"), lax.axis_index("seq")

    def copy(self, half, k):
        to = lax.rem(self.seq + k, 32)
        return pltpu.make_async_remote_copy(
            src_ref=self.out.at[half, to], dst_ref=self.taken.at[half, self.seq],
            send_sem=self.send.at[half, k], recv_sem=self.recv.at[half, k],
            device_id=(self.dp, to), device_id_type=MESH)

    def start(self, half):
        @pl.loop(1, 32)
        def _(k):
            self.copy(half, k).start()

        self.taken[half, self.seq] = self.out[half, self.seq]

    def wait(self, half):
        @pl.loop(1, 32)
        def _(k):
            block = self.taken.at[half, lax.rem(self.seq - k + 32, 32)]
            pltpu.make_async_remote_copy(
                src_ref=block, dst_ref=block, send_sem=self.send.at[half, k], recv_sem=self.recv.at[half, k],
                device_id=(self.dp, lax.rem(self.seq + k, 32)), device_id_type=MESH).wait_recv()

    def drain(self):
        for half in range(2):
            @pl.loop(1, 32)
            def _(k):
                self.copy(half, k).wait_send()


class Reduce:
    def __init__(self, theirs, ours, taken, pieces, plane, total, z_out, z_in, x_out, x_in, sems):
        self.theirs, self.ours, self.taken, self.pieces, self.plane = theirs, ours, taken, pieces, plane
        self.total, self.z_out, self.z_in, self.x_out, self.x_in = total, z_out, z_in, x_out, x_in
        (self.cs, self.cr, self.ps, self.pr, self.zs, self.zr, self.xs, self.xr) = sems
        self.core, self.x, self.y, self.z = place()
        self.holds = jnp.logical_and(self.x < 3, lax.div(self.y, 2) == self.core)
        self.me = self.x * 4 + self.y

    def core_copy(self, part):
        return pltpu.make_async_remote_copy(
            src_ref=self.theirs.at[part], dst_ref=self.taken.at[part],
            send_sem=self.cs.at[part], recv_sem=self.cr.at[part],
            device_id=device(1 - self.core, self.x, self.y, self.z), device_id_type=MESH)

    def core_start(self, mixed_t, grad):
        half = times(mixed_t[1 - self.core], grad)
        for part in range(2):
            for upper in range(2):
                at = 144 * upper + 72 * part
                self.theirs[part, upper] = half[at:at + 72].astype(BF16)
            self.core_copy(part).start()
        half = times(mixed_t[self.core], grad)
        for part in range(2):
            for upper in range(2):
                at = 144 * upper + 72 * part
                self.ours[part, upper] = half[at:at + 72]

    def plane_copy(self, part, k):
        piece = lax.rem(k + self.x + 2 * self.y, 6)
        upper, x = lax.div(piece, 3), lax.rem(piece, 3)
        mine = jnp.logical_and(self.x == x, self.y == self.core * 2 + upper)
        copy = pltpu.make_async_remote_copy(
            src_ref=self.pieces.at[part, upper, x], dst_ref=self.plane.at[part, self.me],
            send_sem=self.ps.at[part, k], recv_sem=self.pr.at[part, self.me],
            device_id=device(self.core, x, self.core * 2 + upper, self.z), device_id_type=MESH)
        return mine, copy

    def plane_start(self, part):
        self.core_copy(part).wait_recv()
        for upper in range(2):
            for x in range(3):
                columns = slice(384 * x, 384 * x + 384)
                self.pieces[part, upper, x] = (
                    self.ours[part, upper, :, columns]
                    + self.taken[part, upper, :, columns].astype(F32)).astype(BF16)

        @pl.loop(0, 6)
        def _(k):
            mine, copy = self.plane_copy(part, k)
            pl.when(jnp.logical_not(mine))(copy.start)

        @pl.when(self.holds)
        def _():
            self.plane[part, self.me] = self.pieces[part, lax.rem(self.y, 2), self.x]

    def z_copy(self, part, k):
        k = lax.rem(k + self.z, 8)
        block = 4 * part + lax.rem(k, 4)
        to = lax.div(k, 4) * 8 + block
        return to != self.z, pltpu.make_async_remote_copy(
            src_ref=self.z_out.at[block], dst_ref=self.z_in.at[self.z],
            send_sem=self.zs.at[part, k], recv_sem=self.zr.at[self.z],
            device_id=device(self.core, self.x, self.y, to), device_id_type=MESH)

    def z_start(self, part):
        @pl.when(self.holds)
        def _():
            @pl.loop(0, 16)
            def _(k):
                @pl.when(k != self.me)
                def _():
                    block = self.plane.at[part, k]
                    pltpu.make_async_remote_copy(
                        src_ref=block, dst_ref=block, send_sem=self.ps.at[part, 0], recv_sem=self.pr.at[part, k],
                        device_id=device(1 - self.core, self.x, self.y, self.z), device_id_type=MESH).wait_recv()

            for r in range(3):
                rows = slice(24 * r, 24 * r + 24)
                sum_rows = self.plane[part, 0, rows].astype(F32)
                for k in range(1, 16):
                    sum_rows = sum_rows + self.plane[part, k, rows].astype(F32)
                self.total[rows] = sum_rows
            for k in range(4):
                self.z_out[4 * part + k] = self.total[18 * k:18 * k + 18, :].astype(BF16)

            @pl.loop(0, 8)
            def _(k):
                away, copy = self.z_copy(part, k)
                pl.when(away)(copy.start)

            @pl.when(lax.div(lax.rem(self.z, 8), 4) == part)
            def _():
                self.z_in[self.z] = self.z_out[lax.rem(self.z, 8)]

    def x_copy(self, k):
        other = lax.div(k, 4)
        return pltpu.make_async_remote_copy(
            src_ref=self.x_out, dst_ref=self.x_in.at[self.x],
            send_sem=self.xs.at[k], recv_sem=self.xr.at[self.x],
            device_id=device(lax.rem(self.core + other, 2), lax.rem(self.x + k, 4), self.y, self.z),
            device_id_type=MESH)

    def x_start(self):
        @pl.when(self.holds)
        def _():
            @pl.loop(0, 16)
            def _(k):
                @pl.when(k != self.z)
                def _():
                    block = self.z_in.at[k]
                    pltpu.make_async_remote_copy(
                        src_ref=block, dst_ref=block, send_sem=self.zs.at[0, 0], recv_sem=self.zr.at[k],
                        device_id=device(1 - self.core, self.x, self.y, self.z), device_id_type=MESH).wait_recv()

            sum_rows = self.z_in[0].astype(F32)
            for k in range(1, 16):
                sum_rows = sum_rows + self.z_in[k].astype(F32)
            self.x_out[...] = sum_rows.astype(BF16)

            @pl.loop(1, 8)
            def _(k):
                self.x_copy(k).start()

            self.x_in[self.x] = self.x_out[...]

    def finish(self, out):
        for k in range(3):
            @pl.when(jnp.logical_not(jnp.logical_and(self.holds, self.x == k)))
            def _():
                block = self.x_in.at[k]
                pltpu.make_async_remote_copy(
                    src_ref=block, dst_ref=block, send_sem=self.xs.at[0], recv_sem=self.xr.at[k],
                    device_id=device(1 - self.core, self.x, self.y, self.z), device_id_type=MESH).wait_recv()
            out[:, 384 * k:384 * k + 384] = self.x_in[k].astype(F32)

    def drain(self):
        for part in range(2):
            self.core_copy(part).wait_send()

            @pl.loop(0, 6)
            def _(k):
                mine, copy = self.plane_copy(part, k)
                pl.when(jnp.logical_not(mine))(copy.wait_send)

        @pl.when(self.holds)
        def _():
            for part in range(2):
                @pl.loop(0, 8)
                def _(k):
                    away, copy = self.z_copy(part, k)
                    pl.when(away)(copy.wait_send)

            @pl.loop(1, 8)
            def _(k):
                self.x_copy(k).wait_send()


REDUCE_SCRATCH = [
    pltpu.VMEM((2, 2, 72, 1152), BF16),
    pltpu.VMEM((2, 2, 72, 1152), F32),
    pltpu.VMEM((2, 2, 72, 1152), BF16),
    pltpu.VMEM((2, 2, 3, 72, 384), BF16),
    pltpu.VMEM((2, 16, 72, 384), BF16),
    pltpu.VMEM((72, 384), F32),
    pltpu.VMEM((8, 18, 384), BF16),
    pltpu.VMEM((16, 18, 384), BF16),
    pltpu.VMEM((18, 384), BF16),
    pltpu.VMEM((3, 18, 384), BF16),
]
REDUCE_SEMS = [pltpu.SemaphoreType.DMA(n) for n in ((2,), (2,), (2, 6), (2, 16), (2, 8), (16,), (8,), (3,))]


def times(left, right):
    return jnp.dot(left, right, preferred_element_type=F32)


def times_transposed(left, right):
    return lax.dot_general(left, right, (((1,), (1,)), ((), ())), preferred_element_type=F32)


def transposed_times(left, right):
    return lax.dot_general(left, right, (((0,), (0,)), ((), ())), preferred_element_type=F32)


def split_heads(ref, array):
    for h in range(HEADS):
        ref[h] = array[HEAD * h:HEAD * h + HEAD, :]


def attend(head, queries, keys, values, visible, weights, out):
    scores = transposed_times(keys[head], queries[head]) * SCALE
    if visible is not None:
        scores = jnp.where(visible, scores, -1e30)
    powers = jnp.exp(scores - jnp.max(scores, axis=0, keepdims=True))
    share = powers / jnp.sum(powers, axis=0, keepdims=True)
    weights[head] = share
    out[head] = times(values[head], share.astype(BF16)).astype(BF16)


def attend_grad(head, upstream, queries, keys, values, weights, query_grad, key_grad, value_grad):
    upper, share = upstream[head], weights[head]
    share_grad = transposed_times(values[head], upper)
    score_grad = (share * (share_grad - jnp.sum(share_grad * share, axis=0, keepdims=True))).astype(BF16)
    query_grad[head] = (SCALE * times(keys[head], score_grad)).astype(BF16)
    if key_grad is not None:
        value_grad[head] = times_transposed(upper, share.astype(BF16)).astype(BF16)
        key_grad[head] = (SCALE * times_transposed(queries[head], score_grad)).astype(BF16)


def each_head(go):
    for h in range(HEADS):
        go(h)


def block_pair(
    tokens, qkv, text, length, w_os, w_qc, w_oc, w_qkv, cotangent,
    heads_out, tokens_grad, qkv_grad, os_grad, *scratch,
):
    full, landing, sems, scratch = scratch[0:6], scratch[6:12], scratch[12:20], scratch[20:]
    (to_patches, from_frames, to_frames, from_patches, s1_send, s1_recv, s2_send, s2_recv,
     spatial_w, cross_w, temporal_w, mixed_heads, mixed_t, cross_queries, cross_heads, upstream,
     temporal, temporal_up, temporal_heads, temporal_grads, wide_t, half_t, hidden_ref) = scratch[0:23]
    g = Gather((w_os, w_qc, w_oc, w_qkv), landing, full, sems)
    forth = Switch(to_patches, from_frames, s1_send, s1_recv)
    back = Switch(to_frames, from_patches, s2_send, s2_recv)
    r = Reduce(*scratch[23:33], scratch[33:41])

    barrier = pltpu.get_barrier_semaphore()
    greeted = greet(barrier)
    for b in WEIGHTS:
        g.stage(b)
    pl.semaphore_wait(barrier, greeted)

    def whole(w):
        return full[w][...].reshape(-1, COLUMNS[w])

    def join(heads, into=wide_t):
        for h in range(HEADS):
            into[HEAD * h:HEAD * h + HEAD, :] = heads[h]
        return into[...].T

    def in_halves(transposed, array):
        row = lax.broadcasted_iota(jnp.int32, (128, 128), 0)
        token = lax.broadcasted_iota(jnp.int32, (128, 128), 1)
        if transposed:
            row, token = token, row
        from_row = 4 * lax.div(lax.rem(row, 64), 2) + 2 * lax.div(row, 64) + lax.rem(row, 2)
        moves = jnp.where(from_row == token, 1.0, 0.0).astype(BF16)
        return times(moves, array).astype(BF16)

    def spatial_pair(i):
        for h in (2 * i, 2 * i + 1):
            attend(h, qkv.at[0], qkv.at[1], qkv.at[2], None, spatial_w, mixed_heads)

    for w in (OS, QC, OC):
        g.z_start(w)
    for s in range(3):
        spatial_pair(s)
        for w in (OS, QC, OC):
            g.z_step(w, s)
        if s == 1:
            g.z_start(TQ)
    g.z_start(TK)
    g.z_start(TV)
    spatial_pair(3)
    mixed = join(mixed_heads)
    for half in range(2):
        mixed_t[half] = wide_t[288 * half:288 * half + 288, :]
    for w in (OS, QC, OC):
        g.z_step(w, 3)
    g.z_finish(OS)
    g.pack(OS)
    g.z_finish(QC)
    g.pack(QC)
    g.z_finish(OC)
    g.pack(OC)
    for w in (TQ, TK, TV):
        g.z_step(w, 0)
    g.y_step(OS)
    for w in (TQ, TK, TV):
        g.z_step(w, 1)
    g.y_step(QC)
    g.y_last(OS)
    g.y_step(OC)
    g.x_step(OS)
    g.z_step(TQ, 2)
    g.y_last(QC)
    g.z_step(TK, 2)
    g.x_step(QC)
    g.z_step(TV, 2)
    g.x_last(OS)
    g.y_last(OC)
    g.z_step(TQ, 3)
    g.z_finish(TQ)
    g.pack(TQ)
    g.x_step(OC)
    g.x_last(QC)
    g.finish(OS)
    hidden = (tokens[...].astype(F32) + times(mixed, whole(OS))).astype(BF16)
    hidden_ref[...] = hidden
    for w in (TK, TV):
        g.z_step(w, 3)
        g.z_finish(w)
        g.pack(w)
    g.finish(QC)
    g.x_last(OC)
    split_heads(cross_queries, times(hidden, whole(QC)).astype(BF16).T)
    g.y_step(TQ)
    seen = lax.broadcasted_iota(jnp.int32, (128, 128), 0) < length[0]
    each_head(lambda h: attend(h, cross_queries, text.at[0], text.at[1], seen, cross_w, cross_heads))
    g.finish(OC)
    after = (hidden_ref[...].astype(F32) + times(join(cross_heads), whole(OC))).astype(BF16)
    after = in_halves(False, after)
    for half in range(2):
        to_patches[half] = after[64 * half:64 * half + 64, :].reshape(32, 2, 1152)
        forth.start(half)
    g.y_step(TK)
    g.y_last(TQ)
    g.x_step(TQ)
    g.y_step(TV)
    g.y_last(TK)
    g.x_last(TQ)
    g.x_step(TK)
    g.y_last(TV)
    g.x_step(TV)
    g.x_last(TK)
    g.x_last(TV)
    for half in range(2):
        split_heads(temporal_up.at[half], cotangent[:, 2 * half:2 * half + 2, :].reshape(64, 576).T)
    for w in (TQ, TK, TV):
        g.finish(w)

    same = (lax.rem(lax.broadcasted_iota(jnp.int32, (64, 64), 0), 2)
            == lax.rem(lax.broadcasted_iota(jnp.int32, (64, 64), 1), 2))
    for half in range(2):
        forth.wait(half)
        patched = from_frames[half].reshape(64, 1152)
        for i, w in enumerate((TQ, TK, TV)):
            split_heads(temporal.at[i], times(patched, whole(w)).astype(BF16).T)
        for h in range(HEADS):
            attend(h, temporal.at[0], temporal.at[1], temporal.at[2], same, temporal_w, temporal_heads.at[half])
            attend_grad(h, temporal_up.at[half], temporal.at[0], temporal.at[1], temporal.at[2], temporal_w,
                        temporal_grads.at[0], temporal_grads.at[1], temporal_grads.at[2])
        patch_grad = times_transposed(join(temporal_grads.at[0], half_t), whole(TQ))
        for i, w in ((1, TK), (2, TV)):
            patch_grad = patch_grad + times_transposed(join(temporal_grads.at[i], half_t), whole(w))
        to_frames[half] = patch_grad.astype(BF16).reshape(32, 2, 1152)
        back.start(half)
    for half in range(2):
        heads_out[:, 2 * half:2 * half + 2, :] = join(temporal_heads.at[half], half_t).reshape(32, 2, 576)
    g.drain()
    forth.drain()
    back.wait(0)
    back.wait(1)

    after_grad = in_halves(True, from_patches[...].reshape(128, 1152))
    split_heads(upstream, times_transposed(after_grad, whole(OC)).astype(BF16).T)
    each_head(lambda h: attend_grad(
        h, upstream, cross_queries, text.at[0], text.at[1], cross_w, cross_heads, None, None))
    hidden_grad = (after_grad.astype(F32) + times_transposed(join(cross_heads), whole(QC))).astype(BF16)
    tokens_grad[...] = hidden_grad
    r.core_start(mixed_t, hidden_grad)
    split_heads(upstream, times_transposed(hidden_grad, whole(OS)).astype(BF16).T)
    r.plane_start(0)
    r.plane_start(1)
    each_head(lambda h: attend_grad(
        h, upstream, qkv.at[0], qkv.at[1], qkv.at[2], spatial_w, qkv_grad.at[0], qkv_grad.at[1],
        qkv_grad.at[2]))
    r.z_start(0)
    r.z_start(1)
    r.x_start()
    r.finish(os_grad)
    back.drain()
    r.drain()


def hand_on(*refs):
    for k in range(4):
        refs[4 + k][...] = refs[k][...]


def shards(tokens, spatial_qkv, text_kv, text_len, w_os, w_qc, w_oc, w_qkv, cotangent):
    heads = (HEADS, HEAD, 128)
    vmem = pl.BlockSpec(memory_space=pltpu.VMEM)
    dma = pltpu.SemaphoreType.DMA
    results = pl.pallas_call(
        block_pair,
        out_shape=[
            jax.ShapeDtypeStruct((32, 4, 576), BF16),
            jax.ShapeDtypeStruct((128, 1152), BF16),
            jax.ShapeDtypeStruct((3,) + heads, BF16),
            jax.ShapeDtypeStruct((18, 1152), F32),
        ],
        in_specs=[vmem] * 3 + [pl.BlockSpec(memory_space=pltpu.SMEM)] + [vmem] * 5,
        out_specs=[vmem] * 4,
        scratch_shapes=[pltpu.VMEM((4, 8 * rows, columns), BF16) for rows, columns in zip(ROWS, COLUMNS)]
        + [pltpu.VMEM((8, rows, columns), BF16) for rows, columns in zip(ROWS, COLUMNS)]
        + [dma((6, 4))] * 8
        + [pltpu.VMEM((2, 32, 2, 1152), BF16)] * 4 + [dma((2, 32))] * 4
        + [pltpu.VMEM((HEADS, 128, 128), F32)] * 2 + [pltpu.VMEM((HEADS, 64, 64), F32)]
        + [pltpu.VMEM(heads, BF16), pltpu.VMEM((2, 288, 128), BF16)] + [pltpu.VMEM(heads, BF16)] * 3
        + [pltpu.VMEM((k, HEADS, HEAD, 64), BF16) for k in (3, 2, 2, 3)]
        + [pltpu.VMEM((576, 128), BF16), pltpu.VMEM((576, 64), BF16), pltpu.VMEM((128, 1152), BF16)]
        + REDUCE_SCRATCH + REDUCE_SEMS,
        compiler_params=pltpu.CompilerParams(
            collective_id=0, has_side_effects=True, vmem_limit_bytes=56 * 2**20),
        name="block_pair",
    )(
        tokens.reshape(128, 1152),
        jnp.transpose(spatial_qkv[0, 0], (1, 2, 0)).reshape((3,) + heads),
        jnp.transpose(text_kv[0], (1, 2, 0)).reshape((2,) + heads),
        text_len, w_os, w_qc, w_oc, w_qkv,
        cotangent.reshape(32, 4, 576),
    )
    temporal_heads, tokens_grad, qkv_grad, os_grad = pl.pallas_call(
        hand_on,
        out_shape=[jax.ShapeDtypeStruct(r.shape, r.dtype) for r in results],
        in_specs=[vmem] * 4,
        out_specs=[vmem] * 4,
        name="hand_on",
    )(*results)
    return (
        temporal_heads[None],
        tokens_grad[None, None],
        jnp.transpose(qkv_grad.reshape(3, 576, 128), (2, 0, 1))[None, None],
        os_grad,
    )


def solution(mesh):
    placed = (
        P("dp", "seq", None, None),
        P("dp", "seq", None, None, None),
        P("dp", None, None, None),
        P("dp"),
        P("seq", None),
        P("seq", None),
        P("seq", None),
        P("seq", None),
        P("dp", None, "seq", None),
    )
    return jax.shard_map(
        shards,
        mesh=mesh,
        in_specs=placed,
        out_specs=(
            P("dp", None, "seq", None),
            P("dp", "seq", None, None),
            P("dp", "seq", None, None, None),
            P("seq", None),
        ),
        check_vma=False,
    )
```

time: 145 us -> 123 us (0.85)
  Pallas kernels: 139 us -> 121 us
  local copies, waits for them, and re-layouts: 4.06 us -> 0 us
    pallas_call x1, Pallas kernels: 139 us -> 119 us  [shards(): pl.pallas_call(block_pair, out_shape=[jax.ShapeDtypeStruct((32, 4, 576),...]
    unnamed x10 -> x0, local copies, waits for them, and re-layouts: 4.06 us -> none
    pallas_call x0 -> x1, Pallas kernels: none -> 2.16 us  [shards(): pl.pallas_call(hand_on, out_shape=[jax.ShapeDtypeStruct(r.shape, r.dtype)...]
where the time goes in v4:
time: 123 us
  Pallas kernels  121 us (98%)
  between operations  1.29 us (1%)
    pallas_call x1, Pallas kernels, shards(): pl.pallas_call(block_pair, out_shape=[jax.ShapeDtypeStruct((32, 4, 576),...  119 us

profile of v4, /device:TPU:1, one launch (start us, length us, event | category | flops | bytes accessed | tf_op | source)
XLA Modules:
  0.0 122.7 jit_solution(6170036448084311219)
XLA Ops:
  1.3 119.3 %block_pair.1 = (bf16[32,4,576]{2,1,0:T(4,128)(2,1)}, bf16[128,1152]{1,0:T(8,128)(2,1)}, bf16[3,8,72,128]{3,2,1,0:T(8,128)(2,1)}, f32[18,1152]{1,0:T(8,128)}) custom-call(bf16[128,1152]{1,0:T(8,128)(2,1)} %bitcast.20, bf16[3,8,72,128]{3,2,1,0:T(8,128)(2,1)} %bitcast.19, bf16[2,8,72,128]{3,2,1,0:T(8,128)(2,1)} %bitcast.21, s32[1]{0:T(128)S(6)} %copy.13.length, ...), custom_call_target="tpu_custom_call" | custom-call | tf_op jit(solution)/shard_map/block_pair/pallas_call | solution.py:645
  120.5 2.2 %hand_on.1 = (bf16[32,4,576]{2,1,0:T(4,128)(2,1)}, bf16[128,1152]{1,0:T(8,128)(2,1)}, bf16[3,8,72,128]{3,2,1,0:T(8,128)(2,1)}, f32[18,1152]{1,0:T(8,128)}) custom-call(bf16[32,4,576]{2,1,0:T(4,128)(2,1)} %get-tuple-element.12.refs_0_, bf16[128,1152]{1,0:T(8,128)(2,1)} %get-tuple-element.13.refs_1_, bf16[3,8,72,128]{3,2,1,0:T(8,128)(2,1)} %get-tuple-element.14.refs_2_, ...), custom_call_target="tpu_custom_call" | custom-call | tf_op jit(solution)/shard_map/hand_on/pallas_call | solution.py:674

commit v5 on v4

--- a/solution.py
+++ b/solution.py
@@ -29,32 +29,30 @@
     return ((x * 2 + lax.div(z, 8)) * 2 + core, y * 8 + lax.rem(z, 8))
 
 
-def greet(barrier):
-    core, x, y, z = place()
-
-    def signal(*to):
-        pl.semaphore_signal(barrier, inc=1, device_id=device(*to), device_id_type=MESH)
-
-    @pl.loop(1, 16)
-    def _(k):
-        signal(core, x, y, lax.rem(z + k, 16))
-
-    @pl.loop(0, 4)
-    def _(k):
-        signal(1 - core, lax.rem(x + k, 4), y, z)
-
-    for k in range(1, 4):
-        side = lax.rem(y + k, 4)
-
-        @pl.loop(0, 8)
-        def _(j):
-            signal(core, x, side, lax.div(z, 8) * 8 + j)
-
-        for j in range(4):
-            if j:
-                signal(core, lax.rem(x + j, 4), side, z)
-        signal(core, lax.rem(x + k, 4), y, z)
-    return 55
+class Roll:
+    def __init__(self, heard):
+        self.heard = heard
+        core, x, y, z = place()
+        along_z = lambda n: device(core, x, y, lax.rem(z + n + 16, 16))
+        along_y = lambda n: device(core, x, lax.rem(y + n + 4, 4), z)
+        along_x = lambda n: device(core, lax.rem(x + n + 4, 4), y, z)
+        other = device(1 - core, x, y, z)
+        self.near = (along_z(1), along_z(-1), along_y(1), along_y(-1), along_x(1), along_x(-1), other)
+        self.rounds = (
+            (along_z(1), along_z(-1)), (along_z(2), along_z(-2)), (along_z(4), along_z(-4)),
+            (along_y(1), along_y(-1)), (along_y(2),), (along_x(1), along_x(-1)), (along_x(2),), (other,))
+
+    def greet(self, barrier):
+        for d in self.near:
+            pl.semaphore_signal(barrier, inc=1, device_id=d, device_id_type=MESH)
+        return len(self.near)
+
+    def call(self, k):
+        if k:
+            pl.semaphore_wait(self.heard.at[k - 1], len(self.rounds[k - 1]))
+        if k < len(self.rounds):
+            for d in self.rounds[k]:
+                pl.semaphore_signal(self.heard.at[k], inc=1, device_id=d, device_id_type=MESH)
 
 
 class Gather:
@@ -485,7 +483,8 @@
     r = Reduce(*scratch[23:33], scratch[33:41])
 
     barrier = pltpu.get_barrier_semaphore()
-    greeted = greet(barrier)
+    roll = Roll(scratch[41])
+    greeted = roll.greet(barrier)
     for b in WEIGHTS:
         g.stage(b)
     pl.semaphore_wait(barrier, greeted)
@@ -513,10 +512,12 @@
 
     for w in (OS, QC, OC):
         g.z_start(w)
+    roll.call(0)
     for s in range(3):
         spatial_pair(s)
         for w in (OS, QC, OC):
             g.z_step(w, s)
+        roll.call(s + 1)
         if s == 1:
             g.z_start(TQ)
     g.z_start(TK)
@@ -533,19 +534,23 @@
     g.pack(QC)
     g.z_finish(OC)
     g.pack(OC)
+    roll.call(4)
     for w in (TQ, TK, TV):
         g.z_step(w, 0)
     g.y_step(OS)
     for w in (TQ, TK, TV):
         g.z_step(w, 1)
     g.y_step(QC)
+    roll.call(5)
     g.y_last(OS)
     g.y_step(OC)
     g.x_step(OS)
+    roll.call(6)
     g.z_step(TQ, 2)
     g.y_last(QC)
     g.z_step(TK, 2)
     g.x_step(QC)
+    roll.call(7)
     g.z_step(TV, 2)
     g.x_last(OS)
     g.y_last(OC)
@@ -562,6 +567,7 @@
         g.z_finish(w)
         g.pack(w)
     g.finish(QC)
+    roll.call(8)
     g.x_last(OC)
     split_heads(cross_queries, times(hidden, whole(QC)).astype(BF16).T)
     g.y_step(TQ)
@@ -660,7 +666,7 @@
         + [pltpu.VMEM(heads, BF16), pltpu.VMEM((2, 288, 128), BF16)] + [pltpu.VMEM(heads, BF16)] * 3
         + [pltpu.VMEM((k, HEADS, HEAD, 64), BF16) for k in (3, 2, 2, 3)]
         + [pltpu.VMEM((576, 128), BF16), pltpu.VMEM((576, 64), BF16), pltpu.VMEM((128, 1152), BF16)]
-        + REDUCE_SCRATCH + REDUCE_SEMS,
+        + REDUCE_SCRATCH + REDUCE_SEMS + [pltpu.SemaphoreType.REGULAR((8,))],
         compiler_params=pltpu.CompilerParams(
             collective_id=0, has_side_effects=True, vmem_limit_bytes=56 * 2**20),
         name="block_pair",

time: 123 us -> 119 us (0.967)
  Pallas kernels: 121 us -> 117 us
    pallas_call x1, Pallas kernels: 119 us -> 115 us  [shards(): pl.pallas_call(block_pair, out_shape=[jax.ShapeDtypeStruct((32, 4, 576),...]
where the time goes in v5:
time: 119 us
  Pallas kernels  117 us (98%)
  between operations  1.29 us (1%)
    pallas_call x1, Pallas kernels, shards(): pl.pallas_call(block_pair, out_shape=[jax.ShapeDtypeStruct((32, 4, 576),...  115 us

profile of v5, /device:TPU:1, one launch (start us, length us, event | category | flops | bytes accessed | tf_op | source)
XLA Modules:
  0.0 118.5 jit_solution(14538387119105797455)
XLA Ops:
  1.3 115.1 %block_pair.1 = (bf16[32,4,576]{2,1,0:T(4,128)(2,1)}, bf16[128,1152]{1,0:T(8,128)(2,1)}, bf16[3,8,72,128]{3,2,1,0:T(8,128)(2,1)}, f32[18,1152]{1,0:T(8,128)}) custom-call(bf16[128,1152]{1,0:T(8,128)(2,1)} %bitcast.20, bf16[3,8,72,128]{3,2,1,0:T(8,128)(2,1)} %bitcast.19, bf16[2,8,72,128]{3,2,1,0:T(8,128)(2,1)} %bitcast.21, s32[1]{0:T(128)S(6)} %copy.13.length, ...), custom_call_target="tpu_custom_call" | custom-call | tf_op jit(solution)/shard_map/block_pair/pallas_call | solution.py:651
  116.4 2.2 %hand_on.1 = (bf16[32,4,576]{2,1,0:T(4,128)(2,1)}, bf16[128,1152]{1,0:T(8,128)(2,1)}, bf16[3,8,72,128]{3,2,1,0:T(8,128)(2,1)}, f32[18,1152]{1,0:T(8,128)}) custom-call(bf16[32,4,576]{2,1,0:T(4,128)(2,1)} %get-tuple-element.12.refs_0_, bf16[128,1152]{1,0:T(8,128)(2,1)} %get-tuple-element.13.refs_1_, bf16[3,8,72,128]{3,2,1,0:T(8,128)(2,1)} %get-tuple-element.14.refs_2_, ...), custom_call_target="tpu_custom_call" | custom-call | tf_op jit(solution)/shard_map/hand_on/pallas_call | solution.py:680

commit v6 on v5

--- a/solution.py
+++ b/solution.py
@@ -470,20 +470,25 @@
 
 
 def block_pair(
-    tokens, qkv, text, length, w_os, w_qc, w_oc, w_qkv, cotangent,
+    tokens_in, qkv_in, text_in, length, w_os, w_qc, w_oc, w_qkv, cotangent_in,
     heads_out, tokens_grad, qkv_grad, os_grad, *scratch,
 ):
+    tokens, qkv, text, cotangent, brought = scratch[-5:]
+    fetch = [pltpu.make_async_copy(source, target, brought.at[k]) for k, (source, target) in enumerate(
+        ((qkv_in, qkv), (tokens_in, tokens), (text_in, text), (cotangent_in, cotangent)))]
+    for copy in fetch:
+        copy.start()
     full, landing, sems, scratch = scratch[0:6], scratch[6:12], scratch[12:20], scratch[20:]
     (to_patches, from_frames, to_frames, from_patches, s1_send, s1_recv, s2_send, s2_recv,
-     spatial_w, cross_w, temporal_w, mixed_heads, mixed_t, cross_queries, cross_heads, upstream,
-     temporal, temporal_up, temporal_heads, temporal_grads, wide_t, half_t, hidden_ref) = scratch[0:23]
+     spatial_w, cross_w, temporal_w, mixed_heads, mixed_t, cross_queries, cross_heads, cross_up, upstream,
+     temporal, temporal_up, temporal_heads, temporal_grads, wide_t, half_t, hidden_ref) = scratch[0:24]
     g = Gather((w_os, w_qc, w_oc, w_qkv), landing, full, sems)
     forth = Switch(to_patches, from_frames, s1_send, s1_recv)
     back = Switch(to_frames, from_patches, s2_send, s2_recv)
-    r = Reduce(*scratch[23:33], scratch[33:41])
+    r = Reduce(*scratch[24:34], scratch[34:42])
 
     barrier = pltpu.get_barrier_semaphore()
-    roll = Roll(scratch[41])
+    roll = Roll(scratch[42])
     greeted = roll.greet(barrier)
     for b in WEIGHTS:
         g.stage(b)
@@ -513,6 +518,7 @@
     for w in (OS, QC, OC):
         g.z_start(w)
     roll.call(0)
+    fetch[0].wait()
     for s in range(3):
         spatial_pair(s)
         for w in (OS, QC, OC):
@@ -524,8 +530,11 @@
     g.z_start(TV)
     spatial_pair(3)
     mixed = join(mixed_heads)
+    mixed_in_halves = in_halves(False, mixed).T
     for half in range(2):
-        mixed_t[half] = wide_t[288 * half:288 * half + 288, :]
+        mixed_t[half] = mixed_in_halves[288 * half:288 * half + 288, :]
+    for copy in fetch[1:]:
+        copy.wait()
     for w in (OS, QC, OC):
         g.z_step(w, 3)
     g.z_finish(OS)
@@ -561,6 +570,7 @@
     g.x_last(QC)
     g.finish(OS)
     hidden = (tokens[...].astype(F32) + times(mixed, whole(OS))).astype(BF16)
+    hidden = in_halves(False, hidden)
     hidden_ref[...] = hidden
     for w in (TK, TV):
         g.z_step(w, 3)
@@ -569,15 +579,18 @@
     g.finish(QC)
     roll.call(8)
     g.x_last(OC)
-    split_heads(cross_queries, times(hidden, whole(QC)).astype(BF16).T)
+    queries = times(hidden, whole(QC)).astype(BF16)
     g.y_step(TQ)
-    seen = lax.broadcasted_iota(jnp.int32, (128, 128), 0) < length[0]
-    each_head(lambda h: attend(h, cross_queries, text.at[0], text.at[1], seen, cross_w, cross_heads))
+    seen = lax.broadcasted_iota(jnp.int32, (128, 64), 0) < length[0]
+    for half in range(2):
+        split_heads(cross_queries.at[half], queries[64 * half:64 * half + 64, :].T)
+        each_head(lambda h: attend(
+            h, cross_queries.at[half], text.at[0], text.at[1], seen, cross_w.at[half], cross_heads.at[half]))
     g.finish(OC)
-    after = (hidden_ref[...].astype(F32) + times(join(cross_heads), whole(OC))).astype(BF16)
-    after = in_halves(False, after)
     for half in range(2):
-        to_patches[half] = after[64 * half:64 * half + 64, :].reshape(32, 2, 1152)
+        after = (hidden_ref[64 * half:64 * half + 64, :].astype(F32)
+                 + times(join(cross_heads.at[half], half_t), whole(OC))).astype(BF16)
+        to_patches[half] = after.reshape(32, 2, 1152)
         forth.start(half)
     g.y_step(TK)
     g.y_last(TQ)
@@ -615,19 +628,21 @@
         heads_out[:, 2 * half:2 * half + 2, :] = join(temporal_heads.at[half], half_t).reshape(32, 2, 576)
     g.drain()
     forth.drain()
-    back.wait(0)
-    back.wait(1)
-
-    after_grad = in_halves(True, from_patches[...].reshape(128, 1152))
-    split_heads(upstream, times_transposed(after_grad, whole(OC)).astype(BF16).T)
-    each_head(lambda h: attend_grad(
-        h, upstream, cross_queries, text.at[0], text.at[1], cross_w, cross_heads, None, None))
-    hidden_grad = (after_grad.astype(F32) + times_transposed(join(cross_heads), whole(QC))).astype(BF16)
-    tokens_grad[...] = hidden_grad
+    for half in range(2):
+        back.wait(half)
+        after_grad = from_patches[half].reshape(64, 1152)
+        split_heads(cross_up, times_transposed(after_grad, whole(OC)).astype(BF16).T)
+        each_head(lambda h: attend_grad(
+            h, cross_up, cross_queries.at[half], text.at[0], text.at[1], cross_w.at[half], cross_heads.at[half],
+            None, None))
+        hidden_ref[64 * half:64 * half + 64, :] = (
+            after_grad.astype(F32) + times_transposed(join(cross_heads.at[half], half_t), whole(QC))).astype(BF16)
+    hidden_grad = hidden_ref[...]
     r.core_start(mixed_t, hidden_grad)
-    split_heads(upstream, times_transposed(hidden_grad, whole(OS)).astype(BF16).T)
+    split_heads(upstream, in_halves(True, times_transposed(hidden_grad, whole(OS)).astype(BF16)).T)
     r.plane_start(0)
     r.plane_start(1)
+    tokens_grad[...] = in_halves(True, hidden_ref[...])
     each_head(lambda h: attend_grad(
         h, upstream, qkv.at[0], qkv.at[1], qkv.at[2], spatial_w, qkv_grad.at[0], qkv_grad.at[1],
         qkv_grad.at[2]))
@@ -648,6 +663,7 @@
     heads = (HEADS, HEAD, 128)
     vmem = pl.BlockSpec(memory_space=pltpu.VMEM)
     dma = pltpu.SemaphoreType.DMA
+    anywhere = pl.BlockSpec(memory_space=pl.ANY)
     results = pl.pallas_call(
         block_pair,
         out_shape=[
@@ -656,17 +672,20 @@
             jax.ShapeDtypeStruct((3,) + heads, BF16),
             jax.ShapeDtypeStruct((18, 1152), F32),
         ],
-        in_specs=[vmem] * 3 + [pl.BlockSpec(memory_space=pltpu.SMEM)] + [vmem] * 5,
+        in_specs=[anywhere] * 3 + [pl.BlockSpec(memory_space=pltpu.SMEM)] + [vmem] * 4 + [anywhere],
         out_specs=[vmem] * 4,
         scratch_shapes=[pltpu.VMEM((4, 8 * rows, columns), BF16) for rows, columns in zip(ROWS, COLUMNS)]
         + [pltpu.VMEM((8, rows, columns), BF16) for rows, columns in zip(ROWS, COLUMNS)]
         + [dma((6, 4))] * 8
         + [pltpu.VMEM((2, 32, 2, 1152), BF16)] * 4 + [dma((2, 32))] * 4
-        + [pltpu.VMEM((HEADS, 128, 128), F32)] * 2 + [pltpu.VMEM((HEADS, 64, 64), F32)]
-        + [pltpu.VMEM(heads, BF16), pltpu.VMEM((2, 288, 128), BF16)] + [pltpu.VMEM(heads, BF16)] * 3
+        + [pltpu.VMEM((HEADS, 128, 128), F32), pltpu.VMEM((2, HEADS, 128, 64), F32), pltpu.VMEM((HEADS, 64, 64), F32)]
+        + [pltpu.VMEM(heads, BF16), pltpu.VMEM((2, 288, 128), BF16)]
+        + [pltpu.VMEM((2, HEADS, HEAD, 64), BF16)] * 2 + [pltpu.VMEM((HEADS, HEAD, 64), BF16), pltpu.VMEM(heads, BF16)]
         + [pltpu.VMEM((k, HEADS, HEAD, 64), BF16) for k in (3, 2, 2, 3)]
         + [pltpu.VMEM((576, 128), BF16), pltpu.VMEM((576, 64), BF16), pltpu.VMEM((128, 1152), BF16)]
-        + REDUCE_SCRATCH + REDUCE_SEMS + [pltpu.SemaphoreType.REGULAR((8,))],
+        + REDUCE_SCRATCH + REDUCE_SEMS + [pltpu.SemaphoreType.REGULAR((8,))]
+        + [pltpu.VMEM((128, 1152), BF16), pltpu.VMEM((3,) + heads, BF16), pltpu.VMEM((2,) + heads, BF16),
+           pltpu.VMEM((32, 4, 576), BF16), dma((4,))],
         compiler_params=pltpu.CompilerParams(
             collective_id=0, has_side_effects=True, vmem_limit_bytes=56 * 2**20),
         name="block_pair",

time: 119 us -> 118 us (level)
  no operation moved by 1% of the time
where the time goes in v6:
time: 118 us
  Pallas kernels  116 us (98%)
  between operations  1.29 us (1%)
    pallas_call x1, Pallas kernels, shards(): pl.pallas_call(block_pair, out_shape=[jax.ShapeDtypeStruct((32, 4, 576),...  114 us

profile of v6, /device:TPU:1, one launch (start us, length us, event | category | flops | bytes accessed | tf_op | source)
XLA Modules:
  0.0 117.6 jit_solution(3255856576911341860)
XLA Ops:
  1.3 114.1 %block_pair.1 = (bf16[32,4,576]{2,1,0:T(4,128)(2,1)}, bf16[128,1152]{1,0:T(8,128)(2,1)}, bf16[3,8,72,128]{3,2,1,0:T(8,128)(2,1)}, f32[18,1152]{1,0:T(8,128)}) custom-call(bf16[128,1152]{1,0:T(8,128)(2,1)} %bitcast.20, bf16[3,8,72,128]{3,2,1,0:T(8,128)(2,1)} %bitcast.19, bf16[2,8,72,128]{3,2,1,0:T(8,128)(2,1)} %bitcast.21, s32[1]{0:T(128)S(6)} %copy.13.length, ...), custom_call_target="tpu_custom_call" | custom-call | tf_op jit(solution)/shard_map/block_pair/pallas_call | solution.py:667
  115.4 2.2 %hand_on.1 = (bf16[32,4,576]{2,1,0:T(4,128)(2,1)}, bf16[128,1152]{1,0:T(8,128)(2,1)}, bf16[3,8,72,128]{3,2,1,0:T(8,128)(2,1)}, f32[18,1152]{1,0:T(8,128)}) custom-call(bf16[32,4,576]{2,1,0:T(4,128)(2,1)} %get-tuple-element.12.refs_0_, bf16[128,1152]{1,0:T(8,128)(2,1)} %get-tuple-element.13.refs_1_, bf16[3,8,72,128]{3,2,1,0:T(8,128)(2,1)} %get-tuple-element.14.refs_2_, ...), custom_call_target="tpu_custom_call" | custom-call | tf_op jit(solution)/shard_map/hand_on/pallas_call | solution.py:699
